TPU v7x, 256 devices: a whole 4x4x8 slice. The times are simulated.
256 devices in a mesh: dp: 32 (over x, z_hi, core), feat: 8 (over y, z_lo).
Axes of the slice: x: 4, y: 4, z: 8 (z_hi: 4, z_lo: 2; z = z_hi * 2 + z_lo), core: 2. Of those that a mesh axis runs over, the one named last changes fastest.
Arguments:
- view_a: bfloat16 [4096, 8192], P('dp', 'feat'), as said below
- view_b: bfloat16 [4096, 8192], P('dp', 'feat'), as said below
Outputs:
- loss: float32 [], replicated
- grad_a: float32 [4096, 8192], P('dp', 'feat')
- grad_b: float32 [4096, 8192], P('dp', 'feat')
Inputs may be any that keep to these rules, and one draw needn't show every extreme that they name: `view_a`: real-valued projector outputs of order one to ten. `view_b`: real-valued projector outputs of order one to ten.
All inputs are finite; a program needn't handle non-finite values.
Results may differ from a plain program's by a relative error of at most 0.0065.
Values may be sent and summed in bfloat16 or wider, within the bound.
A program may use at most 64 MiB of HBM per device.

v0:
```python
import jax
import jax.numpy as jnp
from jax import lax
from jax.sharding import PartitionSpec as P

lam = 0.0051
eps = 1e-05


def backnorm(upper, normed, rstd, first, second, batch):
    return rstd * (upper - first / batch - normed * (second / batch))


def local(view_a, view_b):
    rows, block = view_a.shape
    n_data = lax.axis_size("dp")
    batch = rows * n_data
    values_a = view_a.astype(jnp.float32)
    values_b = view_b.astype(jnp.float32)
    sums = lax.psum((jnp.sum(values_a, axis=0), jnp.sum(values_b, axis=0)), "dp")
    centered_a = values_a - sums[0] / batch
    centered_b = values_b - sums[1] / batch
    squares = lax.psum(
        (jnp.sum(centered_a * centered_a, axis=0), jnp.sum(centered_b * centered_b, axis=0)), "dp"
    )
    var_a = squares[0] / batch
    var_b = squares[1] / batch
    rstd_a = lax.rsqrt(var_a + eps)
    rstd_b = lax.rsqrt(var_b + eps)
    norm_a = (centered_a * rstd_a).astype(jnp.bfloat16)
    norm_b = (centered_b * rstd_b).astype(jnp.bfloat16)
    a_row = lax.all_gather(norm_a, "feat", axis=1, tiled=True)
    a_cols = lax.all_to_all(a_row, "dp", split_axis=1, concat_axis=0, tiled=True)
    width = a_cols.shape[1]
    contract_rows = (((0,), (0,)), ((), ()))
    b_all = lax.all_gather(norm_b, "dp", axis=0, tiled=True)
    corr = lax.dot_general(a_cols, b_all, contract_rows, preferred_element_type=jnp.float32)
    corr = corr / batch
    feature_a = lax.axis_index("dp") * width + lax.broadcasted_iota(jnp.int32, (width, block), 0)
    feature_b = lax.axis_index("feat") * block + lax.broadcasted_iota(jnp.int32, (width, block), 1)
    on_diag = feature_a == feature_b
    target = jnp.where(on_diag, 1.0, 0.0).astype(jnp.float32)
    weight = jnp.where(on_diag, 1.0, lam).astype(jnp.float32)
    gap = corr - target
    loss = lax.psum(jnp.sum(weight * gap * gap), ("dp", "feat"))
    grad_corr = (2.0 * weight * gap).astype(jnp.bfloat16)
    up_b = lax.psum_scatter(
        jnp.dot(a_cols, grad_corr, preferred_element_type=jnp.float32),
        "dp",
        scatter_dimension=0,
        tiled=True,
    )
    contract_cols = (((1,), (1,)), ((), ()))
    partial_a = lax.dot_general(b_all, grad_corr, contract_cols, preferred_element_type=jnp.float32)
    spread = lax.all_to_all(partial_a, "dp", split_axis=0, concat_axis=1, tiled=True)
    up_a = lax.psum_scatter(spread, "feat", scatter_dimension=1, tiled=True)
    normed_a = norm_a.astype(jnp.float32)
    normed_b = norm_b.astype(jnp.float32)
    moments = lax.psum(
        (
            jnp.sum(up_a, axis=0),
            jnp.sum(up_a * normed_a, axis=0),
            jnp.sum(up_b, axis=0),
            jnp.sum(up_b * normed_b, axis=0),
        ),
        "dp",
    )
    grad_a = backnorm(up_a, normed_a, rstd_a, moments[0], moments[1], batch)
    grad_b = backnorm(up_b, normed_b, rstd_b, moments[2], moments[3], batch)
    return (loss, grad_a, grad_b)


def solution(mesh):
    placed = (P("dp", "feat"), P("dp", "feat"))
    return jax.shard_map(
        local,
        mesh=mesh,
        in_specs=placed,
        out_specs=(P(), P("dp", "feat"), P("dp", "feat")),
        check_vma=False,
    )
```

profile of v0, /device:TPU:1, one launch (start us, length us, event | category | flops | bytes accessed | tf_op | source)
XLA Modules:
  0.0 852.0 jit_solution(17108635142098106681)
XLA Ops:
  7.2 0.0 all-gather.3.cloned.1.call-start
  7.2 1.0 convert_reduce_fusion
  8.2 1.1 copy.7
  9.3 0.1 convert_reduce_fusion.1
  9.5 74.4 %all-reduce.2 = (f32[1024]{0:T(1024)S(1)}, f32[1024]{0:T(1024)S(1)}) all-reduce(f32[1024]{0:T(1024)S(1)} %convert_reduce_fusion.1, f32[1024]{0:T(1024)S(1)} %convert_reduce_fusion), channel_id=1, replica_groups=mesh['dp'=32,'feat'=8] {'dp'}, use_global_device_ids=true, to_apply=%region_1.0 | all-reduce | flops 2048 | bytes 16384 | tf_op jit(solution)/shard_map/psum | solution.py:20
  83.9 1.0 fusion.8
  84.9 0.4 fusion.10
  85.3 76.2 %all-reduce.1 = (f32[1024]{0:T(1024)S(1)}, f32[1024]{0:T(1024)S(1)}) all-reduce(f32[1024]{0:T(1024)S(1)} %fusion.10, f32[1024]{0:T(1024)S(1)} %fusion.8), channel_id=1, replica_groups=mesh['dp'=32,'feat'=8] {'dp'}, use_global_device_ids=true, to_apply=%region_3.0 | all-reduce | flops 2048 | bytes 16384 | tf_op jit(solution)/shard_map/psum | solution.py:23
  161.4 1.0 fusion.11
  162.5 0.0 all-gather.3.cloned.1.call-update
  162.5 0.0 all-gather.5.cloned.1.call-start
  162.6 1.7 fusion.9
  164.3 0.0 all-gather.5.cloned.1.call-update
  164.3 47.2 %all-gather.3.cloned.1.call-done = bf16[128,8192]{0,1:T(8,128)(2,1)} async-done(((bf16[128,1024]{0,1:T(8,128)(2,1)}), bf16[128,8192]{0,1:T(8,128)(2,1)}) %all-gather.3.cloned.1.call-update) | async-done | bytes 2097168 | tf_op jit(solution)/shard_map/all_gather | solution.py:32
  211.6 9.6 %all-to-all-start = ((bf16[128,32,256]{0,2,1:T(8,128)(2,1)}), bf16[128,32,256]{0,2,1:T(8,128)(2,1)S(1)}, u32[]{:S(2)}, u32[]{:S(2)}) async-start(bf16[128,32,256]{0,2,1:T(8,128)(2,1)} %bitcast.16), calls=%async_computation | async-start | bytes 4194304 | tf_op jit(solution)/shard_map/all_to_all | solution.py:33
  221.1 0.0 reduce-scatter.3.cloned.1.call-start
  221.2 59.4 %all-to-all-done = bf16[128,32,256]{0,2,1:T(8,128)(2,1)S(1)} async-done(((bf16[128,32,256]{0,2,1:T(8,128)(2,1)}), bf16[128,32,256]{0,2,1:T(8,128)(2,1)S(1)}, u32[]{:S(2)}, u32[]{:S(2)}) %all-to-all-start) | async-done | bytes 2097184 | tf_op jit(solution)/shard_map/all_to_all | solution.py:33
  280.6 0.0 copy-start.1
  280.6 1.4 copy-done.1
  282.0 3.3 copy.8
  285.2 37.6 %all-gather.5.cloned.1.call-done = bf16[4096,1024]{1,0:T(8,128)(2,1)} async-done(((bf16[128,1024]{1,0:T(8,128)(2,1)}), bf16[4096,1024]{1,0:T(8,128)(2,1)}) %all-gather.5.cloned.1.call-update) | async-done | bytes 8388624 | tf_op jit(solution)/shard_map/all_gather | solution.py:36
  322.8 0.0 copy-start
  322.8 6.6 fusion.3
  329.5 0.0 copy-done
  329.5 2.5 fusion.20
  332.0 105.3 %all_to_all.38 = f32[32,128,256]{2,1,0:T(8,128)} all-to-all(f32[32,128,256]{2,1,0:T(8,128)S(1)} %bitcast.15), channel_id=1, replica_groups=mesh['dp'=32,'feat'=8] {'dp'}, dimensions={0} | all-to-all | bytes 8388608 | tf_op jit(solution)/shard_map/all_to_all | solution.py:55
  437.3 5.6 copy.9
  442.9 0.0 reduce-scatter.3.cloned.1.call-update
  442.9 0.0 reduce-scatter.5.cloned.1.call-start
  442.9 8.2 fusion.18
  451.1 0.0 copy-start.2
  451.1 0.0 reduce-scatter.5.cloned.1.call-update
  451.2 76.7 %psum.67 = f32[]{:T(128)} all-reduce(f32[]{:T(128)} %get-tuple-element.18), channel_id=1, replica_groups=mesh['dp'=32,'feat'=8] {'dp','feat'}, use_global_device_ids=true, to_apply=%region_9.10 | all-reduce | flops 1 | bytes 8 | tf_op jit(solution)/shard_map/psum | solution.py:45
  527.8 7.2 reduce-scatter.3.cloned.1.call-done
  535.1 1.7 fusion.23
  536.8 169.7 %reduce-scatter.5.cloned.1.call-done = f32[128,1024]{1,0:T(8,128)} async-done(((f32[4096,1024]{1,0:T(8,128)}), f32[128,1024]{1,0:T(8,128)}) %reduce-scatter.5.cloned.1.call-update) | async-done | bytes 524304 | tf_op jit(solution)/shard_map/reduce_scatter | solution.py:47
  706.4 0.0 copy-done.2
  706.4 1.2 fusion.22
  707.6 133.3 %all-reduce = (f32[1024]{0:T(1024)S(1)}, f32[1024]{0:T(1024)S(1)}, f32[1024]{0:T(1024)S(1)}, f32[1024]{0:T(1024)S(1)}) all-reduce(f32[1024]{0:T(1024)S(1)} %get-tuple-element.9, f32[1024]{0:T(1024)S(1)} %get-tuple-element.8, f32[1024]{0:T(1024)S(1)} %get-tuple-element.7, ...), channel_id=1, replica_groups=mesh['dp'=32,'feat'=8] {'dp'}, use_global_device_ids=true, to_apply=%region_14.15 | all-reduce | flops 4096 | bytes 32768 | tf_op jit(solution)/shard_map/psum | solution.py:59
  840.9 1.6 fusion.14
  842.5 1.0 copy.10
  843.5 2.0 fusion.17
  (9 shorter events, 0.0 us)
Async XLA Ops:
  7.2 204.4 %all-gather.3.cloned.1.call-start = ((), (), s32[]{:S(2)}) async-start(), calls=%async_computation.4 | async-start | bytes 2359296 | tf_op jit(solution)/shard_map/all_gather | solution.py:32
  162.5 160.3 %all-gather.5.cloned.1.call-start = ((), (), s32[]{:S(2)}) async-start(), calls=%async_computation.5 | async-start | bytes 8650752 | tf_op jit(solution)/shard_map/all_gather | solution.py:36
  211.6 69.0 %all-to-all-start = ((bf16[128,32,256]{0,2,1:T(8,128)(2,1)}), bf16[128,32,256]{0,2,1:T(8,128)(2,1)S(1)}, u32[]{:S(2)}, u32[]{:S(2)}) async-start(bf16[128,32,256]{0,2,1:T(8,128)(2,1)} %bitcast.16), calls=%async_computation | async-start | bytes 4194304 | tf_op jit(solution)/shard_map/all_to_all | solution.py:33
  221.1 313.9 %reduce-scatter.3.cloned.1.call-start = ((), (), s32[]{:S(2)}) async-start(), calls=%async_computation.6 | async-start | bytes 4718592 | tf_op jit(solution)/shard_map/reduce_scatter | solution.py:56
  280.6 1.4 copy-start.1
  322.8 6.7 copy-start
  442.9 263.5 %reduce-scatter.5.cloned.1.call-start = ((), (), s32[]{:S(2)}) async-start(), calls=%async_computation.7 | async-start | bytes 17301504 | tf_op jit(solution)/shard_map/reduce_scatter | solution.py:47
  451.1 255.3 %copy-start.2 = (bf16[128,1024]{1,0:T(8,128)(2,1)S(1)}, bf16[128,1024]{1,0:T(8,128)(2,1)}, u32[]{:S(2)}) copy-start(bf16[128,1024]{1,0:T(8,128)(2,1)} %param.3) | copy-start | bytes 786436
Sparse Core Ops, SparseCore 0:
  162.6 48.8 all-gather.2
  214.7 108.1 all-gather.4
  443.0 91.9 reduce-scatter.2
  539.1 167.2 reduce-scatter.4
where the time goes:
time: 860 us; the launch traced here: 852 us
  blocking collectives  466 us (54%)
  waiting for transfers between devices  321 us (37%)
  matrix products  17.3 us (2%)
  between operations  13.9 us (2%)
  local copies, waits for them, and re-layouts  12.3 us (1%)
  other arithmetic  11.8 us (1%)
  starting transfers between devices  9.74 us (1%)
    reduce_scatter x1, waiting for transfers between devices, local(): lax.psum_scatter(jnp.dot(a_cols, grad_corr, preferred_element_type=jnp.fl...  170 us
    psum x1, blocking collectives, local(): lax.psum((jnp.sum(up_a, axis=0), jnp.sum(up_a * normed_a, axis=0), jnp.su...  133 us
    all_to_all x1, blocking collectives, local(): lax.all_to_all(partial_a, 'dp', split_axis=0, concat_axis=1, tiled=True)  105 us
    psum x1, blocking collectives, local(): loss = lax.psum(jnp.sum(weight * gap * gap), ('dp', 'feat'))  76.7 us
    psum x1, blocking collectives, local(): lax.psum((jnp.sum(centered_a * centered_a, axis=0), jnp.sum(centered_b *...  76.2 us
    psum x1, blocking collectives, local(): lax.psum((jnp.sum(values_a, axis=0), jnp.sum(values_b, axis=0)), 'dp')  74.4 us
    all_to_all x1, waiting for transfers between devices, local(): lax.all_to_all(a_row, 'dp', split_axis=1, concat_axis=0, tiled=True)  59.4 us
    all_gather x1, waiting for transfers between devices, local(): a_row = lax.all_gather(norm_a, 'feat', axis=1, tiled=True)  47.2 us
  transfers between devices with their start and end apart: 5, of which 5 were waited for; matrix products, arithmetic and copies ran while one was open for 2% of the time, Pallas kernels for 0%

commit v1 on v0

v1 whole, which is shorter than its diff:
```python
import jax
import jax.numpy as jnp
from jax import lax
from jax.experimental import pallas as pl
from jax.experimental.pallas import tpu as pltpu
from jax.sharding import PartitionSpec as P

lam = 0.0051
eps = 1e-05
BATCH = 4096.0
WIDTH = 8192.0
MESH = pl.DeviceIdType.MESH
f32 = jnp.float32
bf16 = jnp.bfloat16

OFF = (0, 1, 3, 2)
BACK = {1: 2, 2: 1, 3: 3}

UNITS = ((0, 2, 0), (2, 2, 0), (2, 2, 1), (0, 2, 1), (2, 2, 2), (0, 2, 2), (2, 2, 3), (0, 2, 3))
NU = len(UNITS)


def kernel(
    va, vb, loss_ref, ga_ref, gb_ref,
    raw, nrm, oth, swap, st_x, st_z, st_mine, st_cross, st_out,
    gp, rsy, zs, rz, gf, us, u0, rs_same, rs_diff,
    mom, mx, mz, mc, ly, lz,
    core_s, core_r, gx_s, gx_r, gz_s, gz_r, sx_s, sx_r, sz_s, sz_r, oth_s, oth_r,
    y_s, y_r, z_s, z_r, az_s, az_r, ay_s, ay_r, us_s, us_r, ud_s, ud_r,
    mx_s, mx_r, mz_s, mz_r, m_s, m_r, ly_s, ly_r, lz_s, lz_r,
):
    dp = lax.axis_index("dp")
    ft = lax.axis_index("feat")
    x, zh, core = dp // 8, (dp // 2) % 4, dp % 2
    y, zl = ft // 2, ft % 2

    def dev(ax, az, ac, ay, al):
        return (ax * 8 + az * 2 + ac, ay * 2 + al)

    def xp(d):
        return dev((x + d) % 4, zh, core, y, zl)

    def xq(d):
        return dev((x + d) % 4, zh, 1 - core, y, zl)

    def zp(d):
        return dev(x, (zh + d) % 4, core, y, zl)

    def yp(d):
        return dev(x, zh, core, (y + d) % 4, zl)

    cp = dev(x, zh, 1 - core, y, zl)
    lp = dev(x, zh, core, y, 1 - zl)

    sends = []

    def send(src, dst, ss, rs, to):
        c = pltpu.make_async_remote_copy(
            src_ref=src, dst_ref=dst, send_sem=ss, recv_sem=rs, device_id=to, device_id_type=MESH
        )
        c.start()
        sends.append(c)
        return c

    barrier = pltpu.get_barrier_semaphore()
    peers = [cp, lp]
    for d in (1, 2, 3):
        peers += [xp(d), xq(d), zp(d), yp(d)]
    for p in peers:
        pl.semaphore_signal(barrier, inc=1, device_id=p, device_id_type=MESH)

    first = core == 0
    rows_c = pl.multiple_of(core * 128, 128)
    rows_o = pl.multiple_of((1 - core) * 128, 128)

    def split(i, _):
        r = pl.ds(pl.multiple_of(i * 32, 32), 32)
        a, b = va[r, :], vb[r, :]
        raw[0, pl.ds(pl.multiple_of(core * 128 + i * 32, 32), 32), :] = jnp.where(first, a, b)
        swap[r, :] = jnp.where(first, b, a)
        return 0

    lax.fori_loop(0, 4, split, 0)
    pl.semaphore_wait(barrier, len(peers))

    c = send(swap, raw.at[0, pl.ds(rows_c, 128), :], core_s.at[0], core_r.at[0], cp)
    c.wait_recv()

    lo, hi = pl.ds(0, 128), pl.ds(128, 128)

    def ring(base, ss, rs, to):
        def at(slot, rows):
            return raw.at[base + slot, rows, :]

        own_lo, own_hi = raw.at[0, lo, :], raw.at[0, hi, :]
        return (
            send(own_lo, at(2, lo), ss.at[0], rs.at[0], to(1)),
            send(own_hi, at(1, hi), ss.at[1], rs.at[1], to(3)),
            send(own_hi, at(2, hi), ss.at[2], rs.at[2], to(1)),
            send(own_lo, at(1, lo), ss.at[3], rs.at[3], to(3)),
        )

    def forward(base, ss, rs, to, near):
        near[0].wait_recv()
        a = send(raw.at[base + 2, lo, :], raw.at[base + 3, lo, :], ss.at[4], rs.at[4], to(1))
        near[1].wait_recv()
        b = send(raw.at[base + 1, hi, :], raw.at[base + 3, hi, :], ss.at[5], rs.at[5], to(3))
        return a, b

    gx = ring(0, gx_s, gx_r, xp)
    gz = ring(3, gz_s, gz_r, zp)

    def sums(i, acc):
        v = raw[0, pl.ds(pl.multiple_of(i * 32, 32), 32), :].astype(f32)
        return acc + jnp.sum(v.reshape(4, 8, 1024), axis=0)

    mean = jnp.sum(lax.fori_loop(0, 8, sums, jnp.zeros((8, 1024), f32)), axis=0, keepdims=True) / 256.0

    def squares(i, acc):
        v = raw[0, pl.ds(pl.multiple_of(i * 32, 32), 32), :].astype(f32) - mean
        return acc + jnp.sum((v * v).reshape(4, 8, 1024), axis=0)

    m2 = jnp.sum(lax.fori_loop(0, 8, squares, jnp.zeros((8, 1024), f32)), axis=0, keepdims=True)

    def combine(buf, count):
        means = [buf[k, 0:1, :] for k in range(4)]
        avg = (means[0] + means[1] + means[2] + means[3]) * 0.25
        total = buf[0, 1:2, :] + buf[1, 1:2, :] + buf[2, 1:2, :] + buf[3, 1:2, :]
        dev2 = sum((m - avg) * (m - avg) for m in means)
        return avg, total + count * dev2

    def spread(value_a, value_b, buf, me, ss, rs, to):
        buf[me, 0:1, :] = value_a
        buf[me, 1:2, :] = value_b
        cs = [send(buf.at[me], buf.at[me], ss.at[d - 1], rs.at[d - 1], to(d)) for d in (1, 2, 3)]
        for c in cs:
            c.wait_recv()

    spread(mean, m2, st_x, x, sx_s, sx_r, xp)
    mean, m2 = combine(st_x, 256.0)
    fx = forward(0, gx_s, gx_r, xp, gx)
    spread(mean, m2, st_z, zh, sz_s, sz_r, zp)
    mean, m2 = combine(st_z, 1024.0)
    rstd = lax.rsqrt(m2 / BATCH + eps)
    st_mine[0:1, :] = mean
    st_mine[1:2, :] = rstd
    cst = send(st_mine, st_cross, core_s.at[1], core_r.at[1], cp)

    def normalize(k):
        def step(i, _):
            r = pl.ds(pl.multiple_of(i * 32, 32), 32)
            v = raw[k, r, :].astype(f32)
            nrm[k, r, :] = ((v - st_mine[0:1, :]) * st_mine[1:2, :]).astype(bf16)
            return 0

        lax.fori_loop(0, 8, step, 0)
        return send(nrm.at[k], oth.at[k], oth_s.at[k], oth_r.at[k], cp)

    oc = {0: normalize(0)}
    gx[3].wait_recv()
    oc[1] = normalize(1)
    gx[2].wait_recv()
    oc[2] = normalize(2)
    fz = forward(3, gz_s, gz_r, zp, gz)

    ready = {"x3": False, 1: False, 2: False, 3: False}

    def need_row3():
        if not ready["x3"]:
            ready["x3"] = True
            fx[0].wait_recv()
            fx[1].wait_recv()
            oc[3] = normalize(3)

    def need_col(j):
        if j and not ready[j]:
            ready[j] = True
            if j == 1:
                gz[3].wait_recv()
            elif j == 2:
                gz[2].wait_recv()
            else:
                fz[0].wait_recv()
                fz[1].wait_recv()
            oc[3 + j] = normalize(3 + j)

    piece = pl.multiple_of(y * 64, 64)
    keep = pl.multiple_of(zl * 32, 32)
    give = pl.multiple_of((1 - zl) * 32, 32)
    nt = (((1,), (1,)), ((), ()))
    eye = (
        lax.broadcasted_iota(jnp.int32, (256, 256), 0) == lax.broadcasted_iota(jnp.int32, (256, 256), 1)
    )

    ry, zx, za, ay = {}, {}, {}, {}

    def stage0(u):
        i0, n, j = UNITS[u]
        if i0 + n > 3:
            need_row3()
        need_col(j)
        col = 0 if j == 0 else 3 + j
        for i in range(i0, i0 + n):
            g = lax.dot_general(nrm[i], nrm[col], nt, preferred_element_type=f32)
            if i == 0 and j == 0:
                g = jnp.where(eye, g - WIDTH / 8, g)
            gp[i, j] = g.astype(bf16)
        ry[u] = []
        for d in (2, 1, 3):
            r = pl.ds(pl.multiple_of(((y + d) % 4) * 64, 64), 64)
            ry[u].append(send(
                gp.at[pl.ds(i0, n), j, r, :], rsy.at[d - 1, pl.ds(i0, n), j],
                y_s.at[u, d - 1], y_r.at[u, d - 1], yp(d),
            ))

    def part(i, j, at):
        total = gp[i, j, pl.ds(pl.multiple_of(piece + at, 32), 32), :].astype(f32)
        for d in range(3):
            total = total + rsy[d, i, j, pl.ds(at, 32), :].astype(f32)
        return total

    def stage1(u):
        i0, n, j = UNITS[u]
        for c in ry[u]:
            c.wait_recv()
        for i in range(i0, i0 + n):
            zs[i, j] = part(i, j, give).astype(bf16)
        zx[u] = send(zs.at[pl.ds(i0, n), j], rz.at[pl.ds(i0, n), j], z_s.at[u], z_r.at[u], lp)

    def stage2(u):
        i0, n, j = UNITS[u]
        zx[u].wait_recv()
        r = pl.ds(pl.multiple_of(piece + keep, 32), 32)
        for i in range(i0, i0 + n):
            gf[i, j, r, :] = (part(i, j, keep) + rz[i, j].astype(f32)).astype(bf16)
        at = gf.at[pl.ds(i0, n), j, r, :]
        za[u] = send(at, at, az_s.at[u], az_r.at[u], lp)

    def stage3(u):
        i0, n, j = UNITS[u]
        za[u].wait_recv()
        at = gf.at[pl.ds(i0, n), j, pl.ds(piece, 64), :]
        ay[u] = [send(at, at, ay_s.at[u, d - 1], ay_r.at[u, d - 1], yp(d)) for d in (2, 1, 3)]

    for t in range(NU + 3):
        if t < NU:
            stage0(t)
        if 0 <= t - 1 < NU:
            stage1(t - 1)
        if 0 <= t - 2 < NU:
            stage2(t - 2)
        if 0 <= t - 3 < NU:
            stage3(t - 3)

    def own(i, acc):
        m = nrm[0, pl.ds(pl.multiple_of(core * 128 + i * 32, 32), 32), :].astype(f32)
        o = oth[0, pl.ds(pl.multiple_of(core * 128 + i * 32, 32), 32), :].astype(f32)
        return tuple(
            q + jnp.sum(v.reshape(4, 8, 1024), axis=0) for q, v in zip(acc, (m * o, m, o, m * m, o * o))
        )

    for k in range(7):
        oc[k].wait_recv()
    cst.wait_recv()
    ab, sm, so, mm, oo = (
        jnp.sum(v, axis=0, keepdims=True)
        for v in lax.fori_loop(0, 4, own, (jnp.zeros((8, 1024), f32),) * 5)
    )
    mom[0:1, :] = jnp.zeros((1, 1024), f32)
    mom[1:2, :] = jnp.zeros((1, 1024), f32)
    mom[2:3, :] = ab
    mom[3:4, :] = jnp.where(first, sm, so)
    mom[4:5, :] = jnp.where(first, so, sm)
    mom[5:6, :] = jnp.where(first, mm, oo)
    mom[6:7, :] = jnp.where(first, oo, mm)
    mom[7:8, :] = jnp.zeros((1, 1024), f32)

    def upper(i):
        def tile(t, _):
            cols = pl.ds(pl.multiple_of(t * 256, 256), 256)
            acc = jnp.dot(gf[i, 0], oth[0, :, cols], preferred_element_type=f32)
            for j in (1, 2, 3):
                acc = acc + jnp.dot(gf[i, j], oth[3 + j, :, cols], preferred_element_type=f32)
            us[i, :, cols] = acc.astype(bf16)
            if i == 0:
                u0[:, cols] = acc
            mom[0:1, cols] += jnp.sum(acc, axis=0, keepdims=True)
            mom[1:2, cols] += jnp.sum(acc * oth[i, :, cols].astype(f32), axis=0, keepdims=True)
            return 0

        lax.fori_loop(0, 4, tile, 0)

    same, diff = [], []
    seen = set()
    for i in (3, 2, 1, 0):
        for u in range(NU):
            i0, n, j = UNITS[u]
            if i0 <= i < i0 + n and u not in seen:
                seen.add(u)
                for c in ay[u]:
                    c.wait_recv()
        upper(i)
        if i:
            b = BACK[i]
            same.append(send(
                us.at[i, pl.ds(rows_c, 128), :], rs_same.at[b - 1],
                us_s.at[b - 1], us_r.at[b - 1], xp(OFF[i]),
            ))
            diff.append(send(
                us.at[i, pl.ds(rows_o, 128), :], rs_diff.at[b],
                ud_s.at[b], ud_r.at[b], xq(OFF[i]),
            ))
        else:
            diff.append(send(us.at[0, pl.ds(rows_o, 128), :], rs_diff.at[0], ud_s.at[0], ud_r.at[0], cp))

    def reduce(buf, me, ss, rs, to):
        buf[me] = mom[...]
        cs = [send(buf.at[me], buf.at[me], ss.at[d - 1], rs.at[d - 1], to(d)) for d in (1, 2, 3)]
        for c in cs:
            c.wait_recv()
        mom[...] = buf[0] + buf[1] + buf[2] + buf[3]

    reduce(mx, x, mx_s, mx_r, xp)
    reduce(mz, zh, mz_s, mz_r, zp)
    mc[core] = mom[...]
    send(mc.at[core], mc.at[core], m_s.at[0], m_r.at[0], cp).wait_recv()
    both = mc[0] + mc[1]
    ab, s_a, s_b, aa, bb = (both[k : k + 1, :] for k in range(2, 7))
    first_b, quad_b = mc[0, 0:1, :], mc[0, 1:2, :] + WIDTH * bb
    first_a, quad_a = mc[1, 0:1, :], mc[1, 1:2, :] + WIDTH * aa
    scale = 2.0 * lam / BATCH
    cii = ab / BATCH
    d = (2.0 * (cii - 1.0)).astype(bf16).astype(f32) - 2.0 * lam * cii
    one_a = (scale * (first_a + WIDTH * s_a) + d * s_b) / BATCH
    one_b = (scale * (first_b + WIDTH * s_b) + d * s_a) / BATCH
    two_a = (scale * quad_a + d * ab) / BATCH
    two_b = (scale * quad_b + d * ab) / BATCH

    terms = lam * (quad_b / (BATCH * BATCH) - cii * cii) + (1.0 - cii) * (1.0 - cii)
    ly[y] = jnp.broadcast_to(jnp.sum(terms, axis=1, keepdims=True), (8, 128))
    lc = [send(ly.at[y], ly.at[y], ly_s.at[k - 1], ly_r.at[k - 1], yp(k)) for k in (1, 2, 3)]

    one_m, two_m = jnp.where(first, one_a, one_b), jnp.where(first, two_a, two_b)
    one_c, two_c = jnp.where(first, one_b, one_a), jnp.where(first, two_b, two_a)
    for c in same + diff:
        c.wait_recv()
    for c in lc:
        c.wait_recv()
    lz[zl] = ly[0] + ly[1] + ly[2] + ly[3]
    lzc = send(lz.at[zl], lz.at[zl], lz_s.at[0], lz_r.at[0], lp)

    def finish(i, _):
        r = pl.ds(pl.multiple_of(i * 32, 32), 32)
        at = pl.ds(pl.multiple_of(core * 128 + i * 32, 32), 32)
        m, o = nrm[0, at, :].astype(f32), oth[0, at, :].astype(f32)
        up_c = u0[at, :]
        for k in range(3):
            up_c = up_c + rs_same[k, r, :].astype(f32)
        up_m = rs_diff[0, r, :].astype(f32)
        for k in range(1, 4):
            up_m = up_m + rs_diff[k, r, :].astype(f32)
        up_c = scale * (up_c + WIDTH * o) + d * m
        up_m = scale * (up_m + WIDTH * m) + d * o
        grad_m = st_mine[1:2, :] * (up_m - one_m - m * two_m)
        grad_c = st_cross[1:2, :] * (up_c - one_c - o * two_c)
        ga_ref[r, :] = jnp.where(first, grad_m, grad_c)
        gb_ref[r, :] = jnp.where(first, grad_c, grad_m)
        return 0

    lax.fori_loop(0, 4, finish, 0)
    lzc.wait_recv()
    loss_ref[...] = lz[0] + lz[1]
    for c in sends:
        c.wait_send()


def local(view_a, view_b):
    dma = pltpu.SemaphoreType.DMA
    vm = pltpu.VMEM
    sems = []
    for shape in (
        (2,), (6,), (6,), (3,), (3,), (7,), (NU, 3), (NU,), (NU,), (NU, 3), (3,), (4,),
        (3,), (3,), (1,), (3,), (1,),
    ):
        sems += [dma(shape), dma(shape)]
    vmem = pl.BlockSpec(memory_space=pltpu.VMEM)
    loss, grad_a, grad_b = pl.pallas_call(
        kernel,
        out_shape=(
            jax.ShapeDtypeStruct((8, 128), f32),
            jax.ShapeDtypeStruct((128, 1024), f32),
            jax.ShapeDtypeStruct((128, 1024), f32),
        ),
        in_specs=[vmem, vmem],
        out_specs=(vmem, vmem, vmem),
        scratch_shapes=[
            vm((7, 256, 1024), bf16), vm((7, 256, 1024), bf16), vm((7, 256, 1024), bf16),
            vm((128, 1024), bf16),
            vm((4, 8, 1024), f32), vm((4, 8, 1024), f32), vm((8, 1024), f32), vm((8, 1024), f32),
            vm((8, 1024), f32),
            vm((4, 4, 256, 256), bf16), vm((3, 4, 4, 64, 256), bf16),
            vm((4, 4, 32, 256), bf16), vm((4, 4, 32, 256), bf16),
            vm((4, 4, 256, 256), bf16),
            vm((4, 256, 1024), bf16), vm((256, 1024), f32),
            vm((3, 128, 1024), bf16), vm((4, 128, 1024), bf16),
            vm((8, 1024), f32), vm((4, 8, 1024), f32), vm((4, 8, 1024), f32), vm((2, 8, 1024), f32),
            vm((4, 8, 128), f32), vm((2, 8, 128), f32),
        ] + sems,
        compiler_params=pltpu.CompilerParams(
            collective_id=0, has_side_effects=True, vmem_limit_bytes=48 * 2**20
        ),
        name="twins",
    )(view_a, view_b)
    return loss[0, 0], grad_a, grad_b


def solution(mesh):
    placed = (P("dp", "feat"), P("dp", "feat"))
    return jax.shard_map(
        local,
        mesh=mesh,
        in_specs=placed,
        out_specs=(P(), P("dp", "feat"), P("dp", "feat")),
        check_vma=False,
    )
```

time: 860 us -> 135 us (0.16)
  blocking collectives: 466 us -> 0 us
  waiting for transfers between devices: 321 us -> 0 us
  Pallas kernels: 0 us -> 130 us
  matrix products: 17.3 us -> 0 us
  between operations: 13.9 us -> 0.65 us
  other arithmetic: 11.8 us -> 0 us
  starting transfers between devices: 9.74 us -> 0 us
    psum x4 -> x0, blocking collectives: 360 us -> none  [the longest x1 133 us: local(): lax.psum((jnp.sum(up_a, axis=0), jnp.sum(up_a * normed_a, axis=0), jnp.su...]
    reduce_scatter x2 -> x0, waiting for transfers between devices: 177 us -> none  [the longest x1 170 us: local(): lax.psum_scatter(jnp.dot(a_cols, grad_corr, preferred_element_type=jnp.fl...]
    pallas_call x0 -> x1, Pallas kernels: none -> 130 us  [local(): pl.pallas_call(kernel, out_shape=(jax.ShapeDtypeStruct((8, 128), f32), ja...]
    all_to_all x1 -> x0, blocking collectives: 105 us -> none  [local(): lax.all_to_all(partial_a, 'dp', split_axis=0, concat_axis=1, tiled=True)]
    all_gather x2 -> x0, waiting for transfers between devices: 84.8 us -> none  [the longest x1 47.2 us: local(): a_row = lax.all_gather(norm_a, 'feat', axis=1, tiled=True)]
    all_to_all x1 -> x0, waiting for transfers between devices: 59.4 us -> none  [local(): lax.all_to_all(a_row, 'dp', split_axis=1, concat_axis=0, tiled=True)]
    dot_general x3 -> x0, matrix products: 17.3 us -> none  [the longest x1 8.19 us: local(): jnp.dot(a_cols, grad_corr, preferred_element_type=jnp.float32)]
    all_to_all x1 -> x0, starting transfers between devices: 9.57 us -> none  [local(): lax.all_to_all(a_row, 'dp', split_axis=1, concat_axis=0, tiled=True)]
  transfers between devices with their start and end apart: 5 -> 0, of which waited for: 5 -> 0; matrix products, arithmetic and copies ran while one was open for 2% -> 0% of each run, Pallas kernels for 0% -> 0%
where the time goes in v1:
time: 135 us
  Pallas kernels  130 us (96%)
  local copies, waits for them, and re-layouts  3.99 us (3%)
    pallas_call x1, Pallas kernels, local(): pl.pallas_call(kernel, out_shape=(jax.ShapeDtypeStruct((8, 128), f32), ja...  130 us
    unnamed x6, local copies, waits for them, and re-layouts  3.48 us

profile of v1, /device:TPU:1, one launch (start us, length us, event | category | flops | bytes accessed | tf_op | source)
XLA Modules:
  0.0 134.7 jit_solution(11182358381356168693)
XLA Ops:
  0.6 0.0 copy-start
  0.6 0.9 copy-done
  1.6 0.0 copy-start.1
  1.6 0.9 copy-done.1
  2.5 130.1 %twins.1 = (f32[8,128]{1,0:T(8,128)S(1)}, f32[128,1024]{1,0:T(8,128)S(1)}, f32[128,1024]{1,0:T(8,128)S(1)}) custom-call(bf16[128,1024]{1,0:T(8,128)(2,1)S(1)} %copy-done, bf16[128,1024]{1,0:T(8,128)(2,1)S(1)} %copy-done.1), custom_call_target="tpu_custom_call" | custom-call | tf_op jit(solution)/shard_map/twins/pallas_call | solution.py:387
  132.6 0.5 slice.3
  133.1 0.8 copy.7
  133.9 0.8 copy.8
Async XLA Ops:
  0.6 1.0 copy-start
  1.6 0.9 copy-start.1

commit v2 on v1

v2 whole, which is shorter than its diff:
```python
import jax
import jax.numpy as jnp
from jax import lax
from jax.experimental import pallas as pl
from jax.experimental.pallas import tpu as pltpu
from jax.sharding import PartitionSpec as P

lam = 0.0051
eps = 1e-05
BATCH = 4096.0
WIDTH = 8192.0
MESH = pl.DeviceIdType.MESH
f32 = jnp.float32
bf16 = jnp.bfloat16

OFF = (0, 1, 3, 2)

UNITS = (
    (0, 0), (0, 1), (1, 0), (1, 1), (2, 1), (3, 0), (3, 1), (3, 2),
    (1, 2), (2, 2), (0, 2), (3, 3), (1, 3), (2, 3), (0, 3),
)
NU = len(UNITS)
RING = 11
ORDER = (
    (0, 0), (1, 0), (2, 0), (0, 1), (0, 2), (0, 3), (0, 4), (1, 1), (6, 1), (1, 2),
    (1, 3), (0, 5), (1, 4), (0, 6), (7, 0), (2, 1), (2, 2), (6, 2), (0, 7), (2, 3),
    (1, 5), (0, 8), (0, 9), (2, 4), (1, 6), (0, 10), (3, 0), (6, 3), (1, 7), (2, 5),
    (1, 8), (1, 9), (2, 6), (1, 10), (3, 1), (4, 0), (3, 2), (2, 7), (2, 8), (2, 9),
    (2, 10), (4, 1), (3, 3), (5, 0), (3, 4), (4, 2), (5, 1), (4, 3), (4, 4), (3, 5),
    (0, 11), (5, 2), (0, 12), (3, 6), (0, 13), (3, 7), (0, 14), (3, 8), (5, 3), (7, 1),
    (3, 9), (5, 4), (3, 10), (4, 5), (2, 11), (7, 2), (2, 12), (4, 6), (2, 13), (3, 11),
    (7, 3), (4, 7), (3, 12), (2, 14), (4, 8), (4, 9), (3, 13), (4, 10), (5, 5), (5, 6),
    (3, 14), (5, 11), (5, 7), (5, 12), (5, 8), (5, 9), (5, 13), (5, 10), (5, 14),
)
PARTS = 4


def kernel(
    va_hbm, vb_hbm, loss_ref, ga_ref, gb_ref,
    va, vb, raw, nrm, oth, swap, st_x, st_z, st_mine, st_cross,
    gp, rsy, ps, zs, rz, gf, us, u0, uf, relay, rs_same, rs_diff,
    mom, mc, mx, mz, own, ox, oz, oc2, ly, lz, lx, lsum,
    in_s, core_s, core_r, gx_s, gx_r, gz_s, gz_r, sx_s, sx_r, sz_s, sz_r, oth_s, oth_r,
    y_s, y_r, z_s, z_r, ay_s, ay_r, us_s, us_r, ud_s, ud_r, rl_s, rl_r,
    mx_s, mx_r, mz_s, mz_r, m_s, m_r, lx_s, lx_r, ox_s, ox_r, oz_s, oz_r, o_s, o_r, ly_s, ly_r, lz_s, lz_r,
):
    dp = lax.axis_index("dp")
    ft = lax.axis_index("feat")
    x, zh, core = dp // 8, (dp // 2) % 4, dp % 2
    y, zl = ft // 2, ft % 2

    def dev(ax, az, ac, ay, al):
        return (ax * 8 + az * 2 + ac, ay * 2 + al)

    def xp(d):
        return dev((x + d) % 4, zh, core, y, zl)

    def xq(d):
        return dev((x + d) % 4, zh, 1 - core, y, zl)

    def zp(d):
        return dev(x, (zh + d) % 4, core, y, zl)

    def yp(d):
        return dev(x, zh, core, (y + d) % 4, zl)

    def zq(d):
        return dev(x, (zh + d) % 4, 1 - core, y, zl)

    def yq(d):
        return dev(x, zh, core, (y + d) % 4, 1 - zl)

    cp = dev(x, zh, 1 - core, y, zl)
    lp = dev(x, zh, core, y, 1 - zl)

    sends = []

    def send(src, dst, ss, rs, to):
        c = pltpu.make_async_remote_copy(
            src_ref=src, dst_ref=dst, send_sem=ss, recv_sem=rs, device_id=to, device_id_type=MESH
        )
        c.start()
        sends.append(c)
        return c

    loads = [
        pltpu.make_async_copy(src, dst, in_s.at[k])
        for k, (src, dst) in enumerate(((va_hbm, va), (vb_hbm, vb)))
    ]
    for c in loads:
        c.start()
    barrier = pltpu.get_barrier_semaphore()
    peers = [cp, lp]
    for d in (1, 2, 3):
        peers += [xp(d), xq(d), zp(d), zq(d), yp(d), yq(d)]
    for p in peers:
        pl.semaphore_signal(barrier, inc=1, device_id=p, device_id_type=MESH)

    first = core == 0
    rows_c = pl.multiple_of(core * 128, 128)
    rows_o = pl.multiple_of((1 - core) * 128, 128)

    for c in loads:
        c.wait()

    def split(i, _):
        r = pl.ds(pl.multiple_of(i * 32, 32), 32)
        a, b = va[r, :], vb[r, :]
        raw[0, pl.ds(pl.multiple_of(core * 128 + i * 32, 32), 32), :] = jnp.where(first, a, b)
        swap[r, :] = jnp.where(first, b, a)
        return 0

    lax.fori_loop(0, 4, split, 0)
    pl.semaphore_wait(barrier, len(peers))

    c = send(swap, raw.at[0, pl.ds(rows_c, 128), :], core_s.at[0], core_r.at[0], cp)
    c.wait_recv()

    lo, hi = pl.ds(0, 128), pl.ds(128, 128)
    own_lo, own_hi = raw.at[0, lo, :], raw.at[0, hi, :]

    def ring(next_lo, next_hi, prev_lo, prev_hi, ss, rs, to):
        return (
            send(own_lo, prev_lo, ss.at[0], rs.at[0], to(1)),
            send(own_hi, next_hi, ss.at[1], rs.at[1], to(3)),
            send(own_hi, prev_hi, ss.at[2], rs.at[2], to(1)),
            send(own_lo, next_lo, ss.at[3], rs.at[3], to(3)),
        )

    def forward(prev_lo, next_hi, far, ss, rs, to, near):
        near[0].wait_recv()
        a = send(prev_lo, raw.at[far, lo, :], ss.at[4], rs.at[4], to(1))
        near[1].wait_recv()
        b = send(next_hi, raw.at[far, hi, :], ss.at[5], rs.at[5], to(3))
        return a, b

    def sums(i, acc):
        v = raw[0, pl.ds(pl.multiple_of(i * 32, 32), 32), :].astype(f32)
        return acc + jnp.sum(v.reshape(4, 8, 1024), axis=0)

    mean = jnp.sum(lax.fori_loop(0, 8, sums, jnp.zeros((8, 1024), f32)), axis=0, keepdims=True) / 256.0

    def squares(i, acc):
        v = raw[0, pl.ds(pl.multiple_of(i * 32, 32), 32), :].astype(f32) - mean
        return acc + jnp.sum((v * v).reshape(4, 8, 1024), axis=0)

    m2 = jnp.sum(lax.fori_loop(0, 8, squares, jnp.zeros((8, 1024), f32)), axis=0, keepdims=True)

    def combine(buf, count):
        means = [buf[k, 0:1, :] for k in range(4)]
        avg = (means[0] + means[1] + means[2] + means[3]) * 0.25
        total = buf[0, 1:2, :] + buf[1, 1:2, :] + buf[2, 1:2, :] + buf[3, 1:2, :]
        dev2 = sum((m - avg) * (m - avg) for m in means)
        return avg, total + count * dev2

    def spread(value_a, value_b, buf, me, ss, rs, to):
        buf[me, 0:1, :] = value_a
        buf[me, 1:2, :] = value_b
        return [send(buf.at[me], buf.at[me], ss.at[d - 1], rs.at[d - 1], to(d)) for d in (1, 2, 3)]

    sz = spread(mean, m2, st_z, zh, sz_s, sz_r, zp)
    gz = ring(
        raw.at[5, lo, :], raw.at[4, lo, :], raw.at[4, hi, :], raw.at[5, hi, :], gz_s, gz_r, zp
    )
    for c in sz:
        c.wait_recv()
    mean, m2 = combine(st_z, 256.0)
    sx = spread(mean, m2, st_x, x, sx_s, sx_r, xp)
    gx = ring(
        raw.at[1, lo, :], raw.at[1, hi, :], raw.at[2, lo, :], raw.at[2, hi, :], gx_s, gx_r, xp
    )
    for c in sx:
        c.wait_recv()
    mean, m2 = combine(st_x, 1024.0)
    rstd = lax.rsqrt(m2 / BATCH + eps)
    st_mine[0:1, :] = mean
    st_mine[1:2, :] = rstd
    cst = send(st_mine, st_cross, core_s.at[1], core_r.at[1], cp)

    def normalize(k):
        def step(i, _):
            r = pl.ds(pl.multiple_of(i * 32, 32), 32)
            v = raw[k, r, :].astype(f32)
            nrm[k, r, :] = ((v - st_mine[0:1, :]) * st_mine[1:2, :]).astype(bf16)
            return 0

        lax.fori_loop(0, 8, step, 0)
        return send(nrm.at[k], oth.at[k], oth_s.at[k], oth_r.at[k], cp)

    oc = {0: normalize(0)}
    far = {}

    def forward_x():
        far["x"] = forward(raw.at[2, lo, :], raw.at[1, hi, :], 3, gx_s, gx_r, xp, gx)

    def forward_z(k):
        if k >= PARTS:
            return
        n = 128 // PARTS
        for e, (half, to) in enumerate(((1, 1), (0, 3))):
            if k == 0:
                gz[e].wait_recv()
            src = raw.at[4, pl.ds(half * 128 + k * n, n), :]
            dst = raw.at[6, pl.ds((1 - half) * 128 + k * n, n), :]
            at = 4 + 2 * k + e
            far.setdefault("z", []).append(send(src, dst, gz_s.at[at], gz_r.at[at], zp(to)))

    arrive = {
        1: lambda: gx[3].wait_recv(),
        2: lambda: gx[2].wait_recv(),
        3: lambda: [c.wait_recv() for c in far["x"]],
        4: lambda: [forward_x(), forward_z(0)],
        5: lambda: [gz[2].wait_recv(), gz[3].wait_recv()],
        6: lambda: [c.wait_recv() for c in far["z"]],
    }

    def need(k):
        if k not in oc:
            arrive[k]()
            oc[k] = normalize(k)

    piece = pl.multiple_of(y * 64, 64)
    nt = (((1,), (1,)), ((), ()))
    eye = (
        lax.broadcasted_iota(jnp.int32, (256, 256), 0) == lax.broadcasted_iota(jnp.int32, (256, 256), 1)
    )

    ry, zx, ay = {}, {}, {}
    mine = pl.ds(piece, 64)

    def rows_of(d, at=0, n=64):
        return pl.ds(pl.multiple_of(((y + d) % 4) * 64 + at, 32), n)

    def stage0(u):
        i, j = UNITS[u]
        col = 3 + j if j else 0
        need(col)
        need(i)
        g = lax.dot_general(nrm[i], nrm[col], nt, preferred_element_type=f32)
        if i == 0 and j == 0:
            g = jnp.where(eye, g - WIDTH / 8, g)
        gp[i, j] = g.astype(bf16)
        if u < RING:
            ry[u] = [
                send(gp.at[i, j, rows_of(2, 0, 32), :], rsy.at[2, i, j, pl.ds(0, 32), :],
                     y_s.at[u, 0], y_r.at[u, 0], yp(1)),
                send(gp.at[i, j, rows_of(2, 32, 32), :], rsy.at[2, i, j, pl.ds(32, 32), :],
                     y_s.at[u, 1], y_r.at[u, 1], yp(3)),
            ]
        else:
            ry[u] = [
                send(gp.at[i, j, rows_of(d), :], rsy.at[d - 1, i, j], y_s.at[u, d - 1], y_r.at[u, d - 1], yp(d))
                for d in (2, 1, 3)
            ]

    def relay_y(u):
        i, j = UNITS[u]
        for c in ry[u]:
            c.wait_recv()
        up = rsy[2, i, j, 0:32, :].astype(f32) + gp[i, j, rows_of(1, 0, 32), :].astype(f32)
        ps[0, i, j, 0:32, :] = up.astype(bf16)
        ps[0, i, j, 32:64, :] = gp[i, j, rows_of(1, 32, 32), :]
        down = rsy[2, i, j, 32:64, :].astype(f32) + gp[i, j, rows_of(3, 32, 32), :].astype(f32)
        ps[1, i, j, 0:32, :] = gp[i, j, rows_of(3, 0, 32), :]
        ps[1, i, j, 32:64, :] = down.astype(bf16)
        ry[u] = [
            send(ps.at[k, i, j], rsy.at[k, i, j], y_s.at[u, 2 + k], y_r.at[u, 2 + k], yp(1 + 2 * k))
            for k in range(2)
        ]

    def stage1(u):
        i, j = UNITS[u]
        for c in ry[u]:
            c.wait_recv()
        total = gp[i, j, mine, :].astype(f32)
        for k in range(2 if u < RING else 3):
            total = total + rsy[k, i, j].astype(f32)
        zs[i, j] = total.astype(bf16)
        zx[u] = send(zs.at[i, j], rz.at[i, j], z_s.at[u], z_r.at[u], lp)

    def stage2(u):
        i, j = UNITS[u]
        zx[u].wait_recv()
        gf[i, j, mine, :] = (zs[i, j].astype(f32) + rz[i, j].astype(f32)).astype(bf16)
        at = gf.at[i, j, mine, :]
        ay[u] = [
            send(at, at, ay_s.at[u, d - 1], ay_r.at[u, d - 1], yp(d)) for d in ((1, 3) if u < RING else (2, 1, 3))
        ]

    def pass_y(u):
        i, j = UNITS[u]
        for c in ay[u]:
            c.wait_recv()
        a = gf.at[i, j, rows_of(3, 0, 32), :]
        b = gf.at[i, j, rows_of(1, 32, 32), :]
        ay[u] = [
            send(a, a, ay_s.at[u, 1], ay_r.at[u, 1], yp(1)),
            send(b, b, ay_s.at[u, 3], ay_r.at[u, 3], yp(3)),
        ]

    def step_own(i, acc):
        at = pl.ds(pl.multiple_of(core * 128 + i * 32, 32), 32)
        m, o = nrm[0, at, :].astype(f32), oth[0, at, :].astype(f32)
        return tuple(
            q + jnp.sum(v.reshape(4, 8, 1024), axis=0) for q, v in zip(acc, (m * o, m, o, m * m, o * o))
        )

    def hop(src, buf, me, ss, rs, to):
        buf[me] = src[...]
        return [send(buf.at[me], buf.at[me], ss.at[d - 1], rs.at[d - 1], to(d)) for d in (1, 2, 3)]

    def swap_cores(src, buf, ss, rs):
        buf[core] = src[...]
        return [send(buf.at[core], buf.at[core], ss.at[0], rs.at[0], cp)]

    def gathered(dst, buf, n, cs):
        for c in cs:
            c.wait_recv()
        total = buf[0]
        for k in range(1, n):
            total = total + buf[k]
        dst[...] = total

    pend = {}

    def own0():
        oc[0].wait_recv()
        ab, sm, so, mm, oo = (
            jnp.sum(v, axis=0, keepdims=True)
            for v in lax.fori_loop(0, 4, step_own, (jnp.zeros((8, 1024), f32),) * 5)
        )
        rows = (
            ab, jnp.where(first, sm, so), jnp.where(first, so, sm),
            jnp.where(first, mm, oo), jnp.where(first, oo, mm),
        )
        for k, v in enumerate(rows):
            own[k : k + 1, :] = v
        own[5:8, :] = jnp.zeros((3, 1024), f32)
        pend["own"] = hop(own, oz, zh, oz_s, oz_r, zp)

    def own1():
        gathered(own, oz, 4, pend["own"])
        pend["own"] = swap_cores(own, oc2, o_s, o_r)

    def own2():
        gathered(own, oc2, 2, pend["own"])
        pend["own"] = hop(own, ox, x, ox_s, ox_r, xp)

    def own3():
        gathered(own, ox, 4, pend["own"])

    mom[...] = jnp.zeros((2, 2, 1024), f32)
    tn = (((0,), (0,)), ((), ()))

    def upper(i):
        blocks = [j for j in range(4) if (i, j) in UNITS]

        def tile(t, _):
            cols = pl.ds(pl.multiple_of(t * 256, 256), 256)
            acc = jnp.zeros((256, 256), f32)
            for j in blocks:
                acc = acc + jnp.dot(gf[i, j], oth[3 + j if j else 0, :, cols], preferred_element_type=f32)
            if i == 0:
                acc = acc + lax.dot_general(gf[1, 0], oth[1, :, cols], tn, preferred_element_type=f32)
                u0[:, cols] = acc
            elif i < 3:
                uf[i - 1, :, cols] = acc
            us[i, :, cols] = acc.astype(bf16)
            one = jnp.sum(acc, axis=0, keepdims=True)
            two = jnp.sum(acc * oth[i, :, cols].astype(f32), axis=0, keepdims=True)
            mom[core, 0:1, cols] += one
            mom[core, 1:2, cols] += two
            return 0

        lax.fori_loop(0, 4, tile, 0)

    same, diff = [], []
    got = set()

    def stage3(u):
        for c in ay[u]:
            c.wait_recv()
        got.add(UNITS[u])
        i = UNITS[u][0]
        if not all(v in got for v in UNITS if v[0] == i):
            return
        for j in range(4):
            k = 3 + j if j else 0
            if k in oc and k not in ready:
                ready.add(k)
                if k:
                    oc[k].wait_recv()
        for k in (i, 1):
            if k not in ready:
                ready.add(k)
                oc[k].wait_recv()
        upper(i)
        rows_same, rows_diff = pl.ds(rows_c, 128), pl.ds(rows_o, 128)
        if i == 3:
            relays.append(send(us.at[3, rows_same, :], relay.at[0], rl_s.at[0], rl_r.at[0], xp(1)))
            relays.append(send(us.at[3, rows_diff, :], relay.at[1], rl_s.at[1], rl_r.at[1], xp(3)))
        elif i == 1:
            diff.append(send(us.at[1, rows_diff, :], rs_diff.at[1], ud_s.at[1], ud_r.at[1], xq(1)))
        elif i == 2:
            same.append(send(us.at[2, rows_same, :], rs_same.at[1], us_s.at[1], us_r.at[1], xp(3)))
        else:
            diff.append(send(us.at[0, rows_diff, :], rs_diff.at[0], ud_s.at[0], ud_r.at[0], cp))

    def pass_x(k):
        start = rows_o if k else rows_c
        relays[k].wait_recv()

        def add(t, _):
            r = pl.ds(pl.multiple_of(t * 32, 32), 32)
            at = pl.ds(pl.multiple_of(start + t * 32, 32), 32)
            us[k + 1, at, :] = (uf[k, at, :] + relay[k, r, :].astype(f32)).astype(bf16)
            return 0

        lax.fori_loop(0, 4, add, 0)
        src = us.at[k + 1, pl.ds(start, 128), :]
        if k == 0:
            same.append(send(src, rs_same.at[0], us_s.at[0], us_r.at[0], xp(1)))
        else:
            diff.append(send(src, rs_diff.at[2], ud_s.at[2], ud_r.at[2], xq(3)))

    relays = []
    ready = {0}
    stages = (stage0, relay_y, stage1, stage2, pass_y, stage3)
    owns = (own0, own1, own2, own3)
    for stage, u in ORDER:
        if stage < 6:
            stages[stage](u)
        elif stage == 6:
            forward_z(u)
        else:
            owns[u]()

    mc[core] = mom[core]
    mc_wait = send(mc.at[core], mc.at[core], m_s.at[0], m_r.at[0], cp)
    cst.wait_recv()
    ab, s_a, s_b, aa, bb = (own[k : k + 1, :] for k in range(5))
    scale = 2.0 * lam / BATCH
    cii = ab / BATCH
    d = (2.0 * (cii - 1.0)).astype(bf16).astype(f32) - 2.0 * lam * cii

    norms = WIDTH * (aa + bb) / (BATCH * BATCH)
    pairs = mom[core, 1:2, :] / (BATCH * BATCH)
    terms = 0.5 * lam * pairs + (
        lam * (0.5 * norms - cii * cii) + (1.0 - cii) * (1.0 - cii)
    ) / 32.0
    ly[ft] = jnp.broadcast_to(jnp.sum(terms, axis=1, keepdims=True), (8, 128))
    ly_wait = []
    for k in (1, 2, 3):
        ly_wait.append(send(ly.at[ft], ly.at[ft], ly_s.at[k], ly_r.at[k], yp(k)))
        ly_wait.append(send(ly.at[ft], ly.at[ft], ly_s.at[k + 3], ly_r.at[k + 3], yq(k)))
    ly_wait.append(send(ly.at[ft], ly.at[ft], ly_s.at[0], ly_r.at[0], lp))
    pass_x(0)
    pass_x(1)
    mc_wait.wait_recv()
    mz_wait = hop(mc, mz, zh, mz_s, mz_r, zp)
    lme = zh * 2 + core
    gathered(lz.at[lme], ly, 8, ly_wait)
    lz_wait = []
    for k in (1, 2, 3):
        lz_wait.append(send(lz.at[lme], lz.at[lme], lz_s.at[k], lz_r.at[k], zp(k)))
        lz_wait.append(send(lz.at[lme], lz.at[lme], lz_s.at[k + 3], lz_r.at[k + 3], zq(k)))
    lz_wait.append(send(lz.at[lme], lz.at[lme], lz_s.at[0], lz_r.at[0], cp))
    gathered(mom, mz, 4, mz_wait)
    mx_wait = hop(mom, mx, x, mx_s, mx_r, xp)
    gathered(lsum, lz, 8, lz_wait)
    lx_wait = hop(lsum, lx, x, lx_s, lx_r, xp)
    gathered(mom, mx, 4, mx_wait)

    first_b, quad_b, first_a, quad_a = (mom[c, k : k + 1, :] for c in range(2) for k in range(2))
    one_a = (scale * (first_a + WIDTH * s_a) + d * s_b) / BATCH
    one_b = (scale * (first_b + WIDTH * s_b) + d * s_a) / BATCH
    two_a = (scale * (quad_a + WIDTH * aa) + d * ab) / BATCH
    two_b = (scale * (quad_b + WIDTH * bb) + d * ab) / BATCH
    one_m, two_m = jnp.where(first, one_a, one_b), jnp.where(first, two_a, two_b)
    one_c, two_c = jnp.where(first, one_b, one_a), jnp.where(first, two_b, two_a)
    for c in same + diff:
        c.wait_recv()

    def finish(i, _):
        r = pl.ds(pl.multiple_of(i * 32, 32), 32)
        at = pl.ds(pl.multiple_of(core * 128 + i * 32, 32), 32)
        m, o = nrm[0, at, :].astype(f32), oth[0, at, :].astype(f32)
        up_c = u0[at, :] + rs_same[0, r, :].astype(f32) + rs_same[1, r, :].astype(f32)
        up_m = rs_diff[0, r, :].astype(f32) + rs_diff[1, r, :].astype(f32) + rs_diff[2, r, :].astype(f32)
        up_c = scale * (up_c + WIDTH * o) + d * m
        up_m = scale * (up_m + WIDTH * m) + d * o
        grad_m = st_mine[1:2, :] * (up_m - one_m - m * two_m)
        grad_c = st_cross[1:2, :] * (up_c - one_c - o * two_c)
        ga_ref[r, :] = jnp.where(first, grad_m, grad_c)
        gb_ref[r, :] = jnp.where(first, grad_c, grad_m)
        return 0

    lax.fori_loop(0, 4, finish, 0)
    gathered(lsum, lx, 4, lx_wait)
    loss_ref[...] = lsum[0:1, 0:1]
    for c in sends:
        c.wait_send()


def local(view_a, view_b):
    dma = pltpu.SemaphoreType.DMA
    vm = pltpu.VMEM
    sems = [dma((2,))]
    for shape in (
        (2,), (6,), (4 + 2 * PARTS,), (3,), (3,), (7,), (NU, 4), (NU,), (NU, 4), (2,), (3,), (2,),
        (3,), (3,), (1,), (3,), (3,), (3,), (1,), (7,), (7,),
    ):
        sems += [dma(shape), dma(shape)]
    vmem = pl.BlockSpec(memory_space=pltpu.VMEM)
    loss, grad_a, grad_b = pl.pallas_call(
        kernel,
        out_shape=(
            jax.ShapeDtypeStruct((1, 1), f32),
            jax.ShapeDtypeStruct((128, 1024), f32),
            jax.ShapeDtypeStruct((128, 1024), f32),
        ),
        in_specs=[pl.BlockSpec(memory_space=pl.ANY)] * 2,
        out_specs=(vmem, vmem, vmem),
        scratch_shapes=[
            vm((128, 1024), bf16), vm((128, 1024), bf16),
            vm((7, 256, 1024), bf16), vm((7, 256, 1024), bf16), vm((7, 256, 1024), bf16),
            vm((128, 1024), bf16),
            vm((4, 2, 1024), f32), vm((4, 2, 1024), f32), vm((8, 1024), f32), vm((8, 1024), f32),
            vm((4, 4, 256, 256), bf16), vm((3, 4, 4, 64, 256), bf16), vm((2, 4, 4, 64, 256), bf16),
            vm((4, 4, 64, 256), bf16), vm((4, 4, 64, 256), bf16),
            vm((4, 4, 256, 256), bf16),
            vm((4, 256, 1024), bf16), vm((256, 1024), f32),
            vm((2, 256, 1024), f32), vm((2, 128, 1024), bf16),
            vm((2, 128, 1024), bf16), vm((3, 128, 1024), bf16),
            vm((2, 2, 1024), f32), vm((2, 2, 1024), f32), vm((4, 2, 2, 1024), f32), vm((4, 2, 2, 1024), f32),
            vm((8, 1024), f32), vm((4, 8, 1024), f32), vm((4, 8, 1024), f32), vm((2, 8, 1024), f32),
            vm((8, 8, 128), f32), vm((8, 8, 128), f32), vm((4, 8, 128), f32), vm((8, 128), f32),
        ] + sems,
        compiler_params=pltpu.CompilerParams(
            collective_id=0, has_side_effects=True, vmem_limit_bytes=48 * 2**20
        ),
        name="twins",
    )(view_a, view_b)
    return loss[0, 0], grad_a, grad_b


def solution(mesh):
    placed = (P("dp", "feat"), P("dp", "feat"))
    return jax.shard_map(
        local,
        mesh=mesh,
        in_specs=placed,
        out_specs=(P(), P("dp", "feat"), P("dp", "feat")),
        check_vma=False,
    )
```

time: 135 us -> 101 us (0.75)
  Pallas kernels: 130 us -> 95.3 us
  between operations: 0.65 us -> 2.41 us
    pallas_call x1, Pallas kernels: 130 us -> 95.3 us  [local(): pl.pallas_call(kernel, out_shape=(jax.ShapeDtypeStruct((1, 1), f32), jax....]
where the time goes in v2:
time: 101 us
  Pallas kernels  95.3 us (94%)
  local copies, waits for them, and re-layouts  3.48 us (3%)
  between operations  2.41 us (2%)
    pallas_call x1, Pallas kernels, local(): pl.pallas_call(kernel, out_shape=(jax.ShapeDtypeStruct((1, 1), f32), jax....  95.3 us
    unnamed x6, local copies, waits for them, and re-layouts  3.48 us

profile of v2, /device:TPU:1, one launch (start us, length us, event | category | flops | bytes accessed | tf_op | source)
XLA Modules:
  0.0 101.2 jit_solution(12900225469088635027)
XLA Ops:
  0.6 0.0 copy-start
  0.6 0.9 copy-done
  1.6 0.0 copy-start.1
  1.6 0.9 copy-done.1
  2.5 95.3 %twins.1 = (f32[1,1]{1,0:T(1,128)}, f32[128,1024]{1,0:T(8,128)S(1)}, f32[128,1024]{1,0:T(8,128)S(1)}) custom-call(bf16[128,1024]{1,0:T(8,128)(2,1)S(1)} %copy-done, bf16[128,1024]{1,0:T(8,128)(2,1)S(1)} %copy-done.1), custom_call_target="tpu_custom_call" | custom-call | tf_op jit(solution)/shard_map/twins/pallas_call | solution.py:515
  98.5 0.8 copy.9
  99.3 0.8 copy.10
Async XLA Ops:
  0.6 1.0 copy-start
  1.6 0.9 copy-start.1

commit v3 on v2

v3 whole, which is shorter than its diff:
```python
import jax
import jax.numpy as jnp
from jax import lax
from jax.experimental import pallas as pl
from jax.experimental.pallas import tpu as pltpu
from jax.sharding import PartitionSpec as P

lam = 0.0051
eps = 1e-05
BATCH = 4096.0
WIDTH = 8192.0
MESH = pl.DeviceIdType.MESH
f32 = jnp.float32
bf16 = jnp.bfloat16

OFF = (0, 1, 3, 2)

UNITS = (
    (0, 0), (0, 1), (1, 0), (1, 1), (2, 1), (3, 0), (3, 1), (3, 2),
    (1, 2), (2, 2), (0, 2), (1, 3), (2, 3), (0, 3), (3, 3),
)
NU = len(UNITS)
RING = 11
ORDER = (
    (0, 0), (1, 0), (2, 0), (0, 1), (0, 2), (0, 3), (0, 4), (6, 1), (1, 1), (1, 2),
    (6, 2), (1, 3), (0, 5), (1, 4), (0, 6), (7, 0), (2, 1), (6, 3), (2, 2), (0, 7),
    (2, 3), (1, 5), (6, 4), (2, 4), (8, 0), (1, 6), (3, 0), (0, 8), (6, 5), (8, 1),
    (1, 7), (7, 1), (2, 5), (2, 6), (8, 2), (3, 1), (0, 9), (6, 6), (4, 0), (1, 8),
    (2, 7), (8, 3), (3, 2), (0, 10), (6, 7), (3, 3), (4, 1), (1, 9), (5, 0), (8, 4),
    (2, 8), (3, 4), (4, 2), (1, 10), (4, 3), (8, 5), (5, 1), (3, 5), (2, 9), (3, 6),
    (4, 4), (5, 2), (2, 10), (8, 6), (5, 3), (3, 7), (4, 5), (4, 6), (5, 4), (8, 7),
    (7, 2), (0, 11), (3, 8), (0, 12), (0, 13), (3, 9), (4, 7), (3, 10), (5, 5), (5, 6),
    (2, 11), (0, 14), (4, 8), (2, 12), (2, 13), (3, 11), (4, 9), (5, 7), (4, 10), (3, 12),
    (2, 14), (5, 8), (3, 13), (5, 11), (5, 9), (5, 10), (3, 14), (5, 12), (5, 13), (7, 3),
    (7, 4), (10, 0), (10, 1), (5, 14),
)
POOL = 48
PARTS = 8


def kernel(
    va_hbm, vb_hbm, loss_ref, ga_ref, gb_ref,
    va, vb, raw, nrm, oth, swap, st_x, st_z, st_mine, st_cross,
    gp, rsy, ps, zs, rz, gf, us, u0, uf, relay, rs_same, rs_diff,
    mom, mx, mz, pc, own, ox, oz, oc2, ly, lz, lx, lsum,
    in_s, pool_s, core_s, gx_s, gz_s, oth_s, us_s, ud_s, rl_s,
    core_r, gx_r, gz_r, oth_r, us_r, ud_r, rl_r, y_r, z_r, ay_r,
    sx_r, sz_r, mx_r, mz_r, pc_r, ox_r, oz_r, o_r, ly_r, lz_r, lx_r,
):
    dp = lax.axis_index("dp")
    ft = lax.axis_index("feat")
    x, zh, core = dp // 8, (dp // 2) % 4, dp % 2
    y, zl = ft // 2, ft % 2

    def dev(ax, az, ac, ay, al):
        return (ax * 8 + az * 2 + ac, ay * 2 + al)

    def xp(d):
        return dev((x + d) % 4, zh, core, y, zl)

    def xq(d):
        return dev((x + d) % 4, zh, 1 - core, y, zl)

    def zp(d):
        return dev(x, (zh + d) % 4, core, y, zl)

    def yp(d):
        return dev(x, zh, core, (y + d) % 4, zl)

    def zq(d):
        return dev(x, (zh + d) % 4, 1 - core, y, zl)

    def yq(d):
        return dev(x, zh, core, (y + d) % 4, 1 - zl)

    cp = dev(x, zh, 1 - core, y, zl)
    lp = dev(x, zh, core, y, 1 - zl)

    sends, busy, turn = [], {}, [0]

    def send(src, dst, ss, rs, to):
        slot = None
        if ss is None:
            slot = turn[0] % POOL
            turn[0] += 1
            if slot in busy:
                busy[slot].wait_send()
            ss = pool_s.at[slot]
        c = pltpu.make_async_remote_copy(
            src_ref=src, dst_ref=dst, send_sem=ss, recv_sem=rs, device_id=to, device_id_type=MESH
        )
        c.start()
        if slot is None:
            sends.append(c)
        else:
            busy[slot] = c
        return c

    class Group:
        def __init__(self, buf, rs):
            self.buf, self.rs = buf, rs

        def wait_recv(self):
            pltpu.make_async_remote_copy(
                src_ref=self.buf, dst_ref=self.buf, send_sem=pool_s.at[0], recv_sem=self.rs,
                device_id=cp, device_id_type=MESH,
            ).wait_recv()

    loads = [
        pltpu.make_async_copy(src, dst, in_s.at[k])
        for k, (src, dst) in enumerate(((va_hbm, va), (vb_hbm, vb)))
    ]
    for c in loads:
        c.start()
    barrier = pltpu.get_barrier_semaphore()
    peers = [cp, lp]
    for d in (1, 2, 3):
        peers += [xp(d), xq(d), zp(d), zq(d), yp(d), yq(d)]
    for p in peers:
        pl.semaphore_signal(barrier, inc=1, device_id=p, device_id_type=MESH)

    first = core == 0
    rows_c = pl.multiple_of(core * 128, 128)
    rows_o = pl.multiple_of((1 - core) * 128, 128)

    for c in loads:
        c.wait()

    def split(i, _):
        r = pl.ds(pl.multiple_of(i * 32, 32), 32)
        a, b = va[r, :], vb[r, :]
        raw[0, pl.ds(pl.multiple_of(core * 128 + i * 32, 32), 32), :] = jnp.where(first, a, b)
        swap[r, :] = jnp.where(first, b, a)
        return 0

    lax.fori_loop(0, 4, split, 0)
    pl.semaphore_wait(barrier, len(peers))

    c = send(swap, raw.at[0, pl.ds(rows_c, 128), :], core_s.at[0], core_r.at[0], cp)
    c.wait_recv()

    lo, hi = pl.ds(0, 128), pl.ds(128, 128)
    own_lo, own_hi = raw.at[0, lo, :], raw.at[0, hi, :]

    def ring(next_lo, next_hi, prev_lo, prev_hi, ss, rs, to):
        return (
            send(own_lo, prev_lo, ss.at[0], rs.at[0], to(1)),
            send(own_hi, next_hi, ss.at[1], rs.at[1], to(3)),
            send(own_hi, prev_hi, ss.at[2], rs.at[2], to(1)),
            send(own_lo, next_lo, ss.at[3], rs.at[3], to(3)),
        )

    def forward(prev_lo, next_hi, far, ss, rs, to, near):
        near[0].wait_recv()
        send(prev_lo, raw.at[far, lo, :], ss.at[4], rs.at[4], to(1))
        near[1].wait_recv()
        send(next_hi, raw.at[far, hi, :], ss.at[5], rs.at[4], to(3))
        return [Group(raw.at[far], rs.at[4])]

    def sums(i, acc):
        v = raw[0, pl.ds(pl.multiple_of(i * 32, 32), 32), :].astype(f32)
        return acc + jnp.sum(v.reshape(4, 8, 1024), axis=0)

    mean = jnp.sum(lax.fori_loop(0, 8, sums, jnp.zeros((8, 1024), f32)), axis=0, keepdims=True) / 256.0

    def squares(i, acc):
        v = raw[0, pl.ds(pl.multiple_of(i * 32, 32), 32), :].astype(f32) - mean
        return acc + jnp.sum((v * v).reshape(4, 8, 1024), axis=0)

    m2 = jnp.sum(lax.fori_loop(0, 8, squares, jnp.zeros((8, 1024), f32)), axis=0, keepdims=True)

    def combine(buf, count):
        means = [buf[k, 0:1, :] for k in range(4)]
        avg = (means[0] + means[1] + means[2] + means[3]) * 0.25
        total = buf[0, 1:2, :] + buf[1, 1:2, :] + buf[2, 1:2, :] + buf[3, 1:2, :]
        dev2 = sum((m - avg) * (m - avg) for m in means)
        return avg, total + count * dev2

    def spread(value_a, value_b, buf, me, rs, to):
        buf[me, 0:1, :] = value_a
        buf[me, 1:2, :] = value_b
        for d in (1, 2, 3):
            send(buf.at[me], buf.at[me], None, rs.at[0], to(d))
        return [Group(buf.at[0:3], rs.at[0])]

    sz = spread(mean, m2, st_z, zh, sz_r, zp)
    gz = ring(
        raw.at[5, lo, :], raw.at[4, lo, :], raw.at[4, hi, :], raw.at[5, hi, :], gz_s, gz_r, zp
    )
    for c in sz:
        c.wait_recv()
    mean, m2 = combine(st_z, 256.0)
    sx = spread(mean, m2, st_x, x, sx_r, xp)
    gx = ring(
        raw.at[1, lo, :], raw.at[1, hi, :], raw.at[2, lo, :], raw.at[2, hi, :], gx_s, gx_r, xp
    )
    for c in sx:
        c.wait_recv()
    mean, m2 = combine(st_x, 1024.0)
    rstd = lax.rsqrt(m2 / BATCH + eps)
    st_mine[0:1, :] = mean
    st_mine[1:2, :] = rstd
    cst = send(st_mine, st_cross, core_s.at[1], core_r.at[1], cp)

    def normalize(k):
        def step(i, _):
            r = pl.ds(pl.multiple_of(i * 32, 32), 32)
            v = raw[k, r, :].astype(f32)
            nrm[k, r, :] = ((v - st_mine[0:1, :]) * st_mine[1:2, :]).astype(bf16)
            return 0

        lax.fori_loop(0, 8, step, 0)
        return send(nrm.at[k], oth.at[k], oth_s.at[k], oth_r.at[k], cp)

    oc = {0: normalize(0)}
    far = {}

    def forward_x():
        far["x"] = forward(raw.at[2, lo, :], raw.at[1, hi, :], 3, gx_s, gx_r, xp, gx)

    def forward_z(k):
        if k >= PARTS:
            return
        n = 128 // PARTS
        for e, (half, to) in enumerate(((1, 1), (0, 3))):
            if k == 0:
                gz[e].wait_recv()
            src = raw.at[4, pl.ds(half * 128 + k * n, n), :]
            dst = raw.at[6, pl.ds((1 - half) * 128 + k * n, n), :]
            send(src, dst, gz_s.at[4 + 2 * k + e], gz_r.at[4 + k], zp(to))

    def pass_far(k):
        n = 128 // PARTS
        Group(raw.at[6, pl.ds(0, 2 * n), :], gz_r.at[4 + k]).wait_recv()
        for half in range(2):
            rows = pl.ds(half * 128 + k * n, n)
            send(raw.at[6, rows, :], raw.at[7, rows, :], None, gx_r.at[5], xp(2))

    arrive = {
        1: lambda: gx[3].wait_recv(),
        2: lambda: gx[2].wait_recv(),
        3: lambda: [c.wait_recv() for c in far["x"]],
        4: lambda: [forward_x(), forward_z(0)],
        5: lambda: [gz[2].wait_recv(), gz[3].wait_recv()],
        6: lambda: None,
        7: lambda: Group(raw.at[7], gx_r.at[5]).wait_recv(),
    }

    def need(k):
        if k not in oc:
            arrive[k]()
            oc[k] = normalize(k)

    piece = pl.multiple_of(y * 64, 64)
    nt = (((1,), (1,)), ((), ()))
    eye = (
        lax.broadcasted_iota(jnp.int32, (256, 256), 0) == lax.broadcasted_iota(jnp.int32, (256, 256), 1)
    )

    ry, zx, ay = {}, {}, {}
    mine = pl.ds(piece, 64)

    def rows_of(d, at=0, n=64):
        return pl.ds(pl.multiple_of(((y + d) % 4) * 64 + at, 32), n)

    def blocks_of(u):
        i, j = UNITS[u]
        return (0, 7) if (i, j) == (3, 3) else (i, 3 + j if j else 0)

    def stage0(u):
        i, j = UNITS[u]
        row, col = blocks_of(u)
        need(col)
        need(row)
        g = lax.dot_general(nrm[row], nrm[col], nt, preferred_element_type=f32)
        if i == 0 and j == 0:
            g = jnp.where(eye, g - WIDTH / 8, g)
        gp[i, j] = g.astype(bf16)
        if u < RING:
            for half, to in ((0, 1), (1, 3)):
                src = gp.at[i, j, rows_of(2, half * 32, 32), :]
                send(src, rsy.at[2, i, j, pl.ds(half * 32, 32), :], None, y_r.at[u, 0], yp(to))
            ry[u] = Group(rsy.at[2, i, j], y_r.at[u, 0])
        else:
            for d in (2, 1, 3):
                send(gp.at[i, j, rows_of(d), :], rsy.at[d - 1, i, j], None, y_r.at[u, 1], yp(d))
            ry[u] = Group(rsy.at[:, i, j], y_r.at[u, 1])

    def relay_y(u):
        i, j = UNITS[u]
        ry[u].wait_recv()
        up = rsy[2, i, j, 0:32, :].astype(f32) + gp[i, j, rows_of(1, 0, 32), :].astype(f32)
        ps[0, i, j, 0:32, :] = up.astype(bf16)
        ps[0, i, j, 32:64, :] = gp[i, j, rows_of(1, 32, 32), :]
        down = rsy[2, i, j, 32:64, :].astype(f32) + gp[i, j, rows_of(3, 32, 32), :].astype(f32)
        ps[1, i, j, 0:32, :] = gp[i, j, rows_of(3, 0, 32), :]
        ps[1, i, j, 32:64, :] = down.astype(bf16)
        for k in range(2):
            send(ps.at[k, i, j], rsy.at[k, i, j], None, y_r.at[u, 1], yp(1 + 2 * k))
        ry[u] = Group(rsy.at[0:2, i, j], y_r.at[u, 1])

    def stage1(u):
        i, j = UNITS[u]
        ry[u].wait_recv()
        total = gp[i, j, mine, :].astype(f32)
        for k in range(2 if u < RING else 3):
            total = total + rsy[k, i, j].astype(f32)
        zs[i, j] = total.astype(bf16)
        zx[u] = send(zs.at[i, j], rz.at[i, j], None, z_r.at[u], lp)

    def stage2(u):
        i, j = UNITS[u]
        zx[u].wait_recv()
        gf[i, j, mine, :] = (zs[i, j].astype(f32) + rz[i, j].astype(f32)).astype(bf16)
        at = gf.at[i, j, mine, :]
        send(at, pc.at[u], None, pc_r.at[0], cp)
        for d in (1, 3) if u < RING else (2, 1, 3):
            send(at, at, None, ay_r.at[u, 0], yp(d))
        ay[u] = Group(rsy.at[0:2, i, j] if u < RING else rsy.at[:, i, j], ay_r.at[u, 0])

    def pass_y(u):
        i, j = UNITS[u]
        ay[u].wait_recv()
        a = gf.at[i, j, rows_of(3, 0, 32), :]
        b = gf.at[i, j, rows_of(1, 32, 32), :]
        send(a, a, None, ay_r.at[u, 1], yp(1))
        send(b, b, None, ay_r.at[u, 1], yp(3))
        ay[u] = Group(rsy.at[2, i, j], ay_r.at[u, 1])

    def step_own(i, acc):
        at = pl.ds(pl.multiple_of(core * 128 + i * 32, 32), 32)
        m, o = nrm[0, at, :].astype(f32), oth[0, at, :].astype(f32)
        return tuple(
            q + jnp.sum(v.reshape(4, 8, 1024), axis=0) for q, v in zip(acc, (m * o, m, o, m * m, o * o))
        )

    def hop(src, buf, me, rs, to):
        buf[me] = src[...]
        for d in (1, 2, 3):
            send(buf.at[me], buf.at[me], None, rs.at[0], to(d))
        return [Group(buf.at[0:3], rs.at[0])]

    def swap_cores(src, buf, rs):
        buf[core] = src[...]
        return [send(buf.at[core], buf.at[core], None, rs.at[0], cp)]

    def gathered(dst, buf, n, cs):
        for c in cs:
            c.wait_recv()
        total = buf[0]
        for k in range(1, n):
            total = total + buf[k]
        dst[...] = total

    pend = {}

    def own0():
        oc[0].wait_recv()
        ab, sm, so, mm, oo = (
            jnp.sum(v, axis=0, keepdims=True)
            for v in lax.fori_loop(0, 4, step_own, (jnp.zeros((8, 1024), f32),) * 5)
        )
        rows = (
            ab, jnp.where(first, sm, so), jnp.where(first, so, sm),
            jnp.where(first, mm, oo), jnp.where(first, oo, mm),
        )
        for k, v in enumerate(rows):
            own[k : k + 1, :] = v
        own[5:8, :] = jnp.zeros((3, 1024), f32)
        pend["own"] = hop(own, ox, x, ox_r, xp)

    def own1():
        gathered(own, ox, 4, pend["own"])
        pend["own"] = swap_cores(own, oc2, o_r)

    def own2():
        gathered(own, oc2, 2, pend["own"])
        pend["own"] = hop(own, oz, zh, oz_r, zp)

    def own3():
        gathered(own, oz, 4, pend["own"])

    scale = 2.0 * lam / BATCH

    def loss0():
        Group(pc, pc_r.at[0]).wait_recv()
        acc = jnp.zeros((8, 256), f32)
        for u, (i, j) in enumerate(UNITS):
            g, h = gf[i, j, mine, :].astype(f32), pc[u].astype(f32)
            if i == 0 and j == 0:
                here = lax.broadcasted_iota(jnp.int32, (64, 256), 0) + piece
                here = here == lax.broadcasted_iota(jnp.int32, (64, 256), 1)
                g, h = jnp.where(here, g + WIDTH, g), jnp.where(here, h + WIDTH, h)
            p = jnp.sum((g * h).reshape(8, 8, 256), axis=0)
            acc = acc + (2.0 * p if (i, j) == (1, 0) else p)
        pairs = jnp.sum(jnp.sum(acc, axis=0, keepdims=True), axis=1, keepdims=True) / (BATCH * BATCH)
        cii = own[0:1, :] / BATCH
        terms = jnp.sum((1.0 - cii) * (1.0 - cii) - lam * cii * cii, axis=1, keepdims=True)
        ly[ft] = jnp.broadcast_to(0.25 * lam * pairs + terms / 32.0, (8, 128))
        for k in (1, 2, 3):
            send(ly.at[ft], ly.at[ft], None, ly_r.at[0], yp(k))
            send(ly.at[ft], ly.at[ft], None, ly_r.at[0], yq(k))
        send(ly.at[ft], ly.at[ft], None, ly_r.at[0], lp)

    def loss1():
        lme = zh * 2 + core
        gathered(lz.at[lme], ly, 8, [Group(ly.at[0:7], ly_r.at[0])])
        for k in (1, 2, 3):
            send(lz.at[lme], lz.at[lme], None, lz_r.at[0], zp(k))
            send(lz.at[lme], lz.at[lme], None, lz_r.at[0], zq(k))
        send(lz.at[lme], lz.at[lme], None, lz_r.at[0], cp)

    def loss2():
        gathered(lsum, lz, 8, [Group(lz.at[0:7], lz_r.at[0])])
        pend["loss"] = hop(lsum, lx, x, lx_r, xp)

    mom[...] = jnp.zeros((2, 1024), f32)
    tn = (((0,), (0,)), ((), ()))
    nn = (((1,), (0,)), ((), ()))

    def product(i, terms, store):
        def tile(t, _):
            cols = pl.ds(pl.multiple_of(t * 256, 256), 256)
            acc = jnp.zeros((256, 256), f32)
            for p, q, k, how in terms:
                acc = acc + lax.dot_general(gf[p, q], oth[k, :, cols], how, preferred_element_type=f32)
            mom[0:1, cols] += jnp.sum(acc, axis=0, keepdims=True)
            mom[1:2, cols] += jnp.sum(acc * oth[i, :, cols].astype(f32), axis=0, keepdims=True)
            store(cols, acc)
            return 0

        lax.fori_loop(0, 4, tile, 0)

    def upper(i):
        terms = [(i, j, 3 + j if j else 0, nn) for j in range(4) if (i, j) in UNITS and (i, j) != (3, 3)]

        def store(cols, acc):
            if i == 0:
                u0[:, cols] = acc
            else:
                us[i, :, cols] = acc.astype(bf16)
            if i in (1, 2):
                uf[i - 1, :, cols] = acc

        product(i, terms + [(1, 0, 1, tn)] if i == 0 else terms, store)

    def upper_far():
        def store(cols, acc):
            acc = acc + u0[:, cols]
            u0[:, cols] = acc
            us[0, :, cols] = acc.astype(bf16)

        product(0, [(3, 3, 7, nn)], store)

    same, diff = [], []
    got = set()

    def stage3(u):
        ay[u].wait_recv()
        got.add(UNITS[u])
        i, j = UNITS[u]
        for k in blocks_of(u) + (1,):
            if k not in ready and k in oc:
                ready.add(k)
                oc[k].wait_recv()
        if (i, j) == (3, 3):
            upper_far()
            diff.append(send(us.at[0, pl.ds(rows_o, 128), :], rs_diff.at[0], ud_s.at[0], ud_r.at[0], cp))
            return
        if not all(v in got for v in UNITS if v[0] == i and v != (3, 3)):
            return
        upper(i)
        rows_same, rows_diff = pl.ds(rows_c, 128), pl.ds(rows_o, 128)
        if i == 3:
            relays.append(send(us.at[3, rows_same, :], relay.at[0], rl_s.at[0], rl_r.at[0], xp(1)))
            relays.append(send(us.at[3, rows_diff, :], relay.at[1], rl_s.at[1], rl_r.at[1], xp(3)))
        elif i == 1:
            diff.append(send(us.at[1, rows_diff, :], rs_diff.at[1], ud_s.at[1], ud_r.at[1], xq(1)))
        elif i == 2:
            same.append(send(us.at[2, rows_same, :], rs_same.at[1], us_s.at[1], us_r.at[1], xp(3)))

    def pass_x(k):
        start = rows_o if k else rows_c
        relays[k].wait_recv()

        def add(t, _):
            r = pl.ds(pl.multiple_of(t * 32, 32), 32)
            at = pl.ds(pl.multiple_of(start + t * 32, 32), 32)
            us[k + 1, at, :] = (uf[k, at, :] + relay[k, r, :].astype(f32)).astype(bf16)
            return 0

        lax.fori_loop(0, 4, add, 0)
        src = us.at[k + 1, pl.ds(start, 128), :]
        if k == 0:
            same.append(send(src, rs_same.at[0], us_s.at[0], us_r.at[0], xp(1)))
        else:
            diff.append(send(src, rs_diff.at[2], ud_s.at[2], ud_r.at[2], xq(3)))

    relays = []
    ready = {0}
    stages = (stage0, relay_y, stage1, stage2, pass_y, stage3)
    owns = (own0, own1, own2, own3, loss0)
    for stage, u in ORDER:
        if stage < 6:
            stages[stage](u)
        elif stage == 6:
            forward_z(u)
        elif stage == 8:
            pass_far(u)
        elif stage == 10:
            pass_x(u)
        else:
            owns[u]()

    mz_wait = hop(mom, mz, zh, mz_r, zp)
    cst.wait_recv()
    ab, s_a, s_b, aa, bb = (own[k : k + 1, :] for k in range(5))
    cii = ab / BATCH
    d = (2.0 * (cii - 1.0)).astype(bf16).astype(f32) - 2.0 * lam * cii
    xme = x * 2 + core
    loss1()
    gathered(mx.at[xme], mz, 4, mz_wait)
    for k in (1, 2, 3):
        send(mx.at[xme], mx.at[xme], None, mx_r.at[0], xp(k))
        send(mx.at[xme], mx.at[xme], None, mx_r.at[0], xq(k))
    send(mx.at[xme], mx.at[xme], None, mx_r.at[0], cp)
    loss2()
    Group(mx.at[0:7], mx_r.at[0]).wait_recv()
    b_sums = mx[0] + mx[2] + mx[4] + mx[6]
    a_sums = mx[1] + mx[3] + mx[5] + mx[7]
    first_b, quad_b, first_a, quad_a = b_sums[0:1], b_sums[1:2], a_sums[0:1], a_sums[1:2]
    one_a = (scale * (first_a + WIDTH * s_a) + d * s_b) / BATCH
    one_b = (scale * (first_b + WIDTH * s_b) + d * s_a) / BATCH
    two_a = (scale * (quad_a + WIDTH * aa) + d * ab) / BATCH
    two_b = (scale * (quad_b + WIDTH * bb) + d * ab) / BATCH
    one_m, two_m = jnp.where(first, one_a, one_b), jnp.where(first, two_a, two_b)
    one_c, two_c = jnp.where(first, one_b, one_a), jnp.where(first, two_b, two_a)
    for c in same + diff:
        c.wait_recv()

    def finish(i, _):
        r = pl.ds(pl.multiple_of(i * 32, 32), 32)
        at = pl.ds(pl.multiple_of(core * 128 + i * 32, 32), 32)
        m, o = nrm[0, at, :].astype(f32), oth[0, at, :].astype(f32)
        up_c = u0[at, :] + rs_same[0, r, :].astype(f32) + rs_same[1, r, :].astype(f32)
        up_m = rs_diff[0, r, :].astype(f32) + rs_diff[1, r, :].astype(f32) + rs_diff[2, r, :].astype(f32)
        up_c = scale * (up_c + WIDTH * o) + d * m
        up_m = scale * (up_m + WIDTH * m) + d * o
        grad_m = st_mine[1:2, :] * (up_m - one_m - m * two_m)
        grad_c = st_cross[1:2, :] * (up_c - one_c - o * two_c)
        ga_ref[r, :] = jnp.where(first, grad_m, grad_c)
        gb_ref[r, :] = jnp.where(first, grad_c, grad_m)
        return 0

    lax.fori_loop(0, 4, finish, 0)
    gathered(lsum, lx, 4, pend["loss"])
    loss_ref[...] = lsum[0:1, 0:1]
    for c in sends + list(busy.values()):
        c.wait_send()


def local(view_a, view_b):
    dma = pltpu.SemaphoreType.DMA
    vm = pltpu.VMEM
    sems = [
        dma(shape)
        for shape in (
            (2,), (POOL,), (2,), (6,), (4 + 2 * PARTS,), (8,), (2,), (3,), (2,),
            (2,), (6,), (4 + PARTS,), (8,), (2,), (3,), (2,), (NU, 2), (NU,), (NU, 2),
        )
    ] + [dma((1,))] * 11
    vmem = pl.BlockSpec(memory_space=pltpu.VMEM)
    loss, grad_a, grad_b = pl.pallas_call(
        kernel,
        out_shape=(
            jax.ShapeDtypeStruct((1, 1), f32),
            jax.ShapeDtypeStruct((128, 1024), f32),
            jax.ShapeDtypeStruct((128, 1024), f32),
        ),
        in_specs=[pl.BlockSpec(memory_space=pltpu.HBM)] * 2,
        out_specs=(vmem, vmem, vmem),
        scratch_shapes=[
            vm((128, 1024), bf16), vm((128, 1024), bf16),
            vm((8, 256, 1024), bf16), vm((8, 256, 1024), bf16), vm((8, 256, 1024), bf16),
            vm((128, 1024), bf16),
            vm((4, 2, 1024), f32), vm((4, 2, 1024), f32), vm((8, 1024), f32), vm((8, 1024), f32),
            vm((4, 4, 256, 256), bf16), vm((3, 4, 4, 64, 256), bf16), vm((2, 4, 4, 64, 256), bf16),
            vm((4, 4, 64, 256), bf16), vm((4, 4, 64, 256), bf16),
            vm((4, 4, 256, 256), bf16),
            vm((4, 256, 1024), bf16), vm((256, 1024), f32),
            vm((2, 256, 1024), f32), vm((2, 128, 1024), bf16),
            vm((2, 128, 1024), bf16), vm((3, 128, 1024), bf16),
            vm((2, 1024), f32), vm((8, 2, 1024), f32), vm((4, 2, 1024), f32), vm((NU, 64, 256), bf16),
            vm((8, 1024), f32), vm((4, 8, 1024), f32), vm((4, 8, 1024), f32), vm((2, 8, 1024), f32),
            vm((8, 8, 128), f32), vm((8, 8, 128), f32), vm((4, 8, 128), f32), vm((8, 128), f32),
        ] + sems,
        compiler_params=pltpu.CompilerParams(
            collective_id=0, has_side_effects=True, vmem_limit_bytes=54 * 2**20
        ),
        name="twins",
    )(view_a, view_b)
    return loss[0, 0], grad_a, grad_b


def solution(mesh):
    placed = (P("dp", "feat"), P("dp", "feat"))
    return jax.shard_map(
        local,
        mesh=mesh,
        in_specs=placed,
        out_specs=(P(), P("dp", "feat"), P("dp", "feat")),
        check_vma=False,
    )
```

time: 101 us -> 97 us (0.960)
  Pallas kernels: 95.3 us -> 91.7 us
    pallas_call x1, Pallas kernels: 95.3 us -> 91.7 us  [local(): pl.pallas_call(kernel, out_shape=(jax.ShapeDtypeStruct((1, 1), f32), jax....]
    unnamed x6 -> x4, local copies, waits for them, and re-layouts: 3.48 us -> 2.74 us
where the time goes in v3:
time: 97 us; the launch traced here: 96.8 us
  Pallas kernels  91.7 us (95%)
  local copies, waits for them, and re-layouts  2.74 us (3%)
  between operations  2.41 us (2%)
    pallas_call x1, Pallas kernels, local(): pl.pallas_call(kernel, out_shape=(jax.ShapeDtypeStruct((1, 1), f32), jax....  91.7 us
    unnamed x4, local copies, waits for them, and re-layouts  2.74 us

profile of v3, /device:TPU:1, one launch (start us, length us, event | category | flops | bytes accessed | tf_op | source)
XLA Modules:
  0.0 96.8 jit_solution(15592356854877003893)
XLA Ops:
  0.6 91.7 %twins.1 = (f32[1,1]{1,0:T(1,128)}, f32[128,1024]{1,0:T(8,128)}, f32[128,1024]{1,0:T(8,128)}) custom-call(bf16[128,1024]{1,0:T(8,128)(2,1)} %va_hbm.1, bf16[128,1024]{1,0:T(8,128)(2,1)} %vb_hbm.1), custom_call_target="tpu_custom_call" | custom-call | tf_op jit(solution)/shard_map/twins/pallas_call | solution.py:573
  93.0 0.0 copy-start
  93.0 1.9 %copy.9 = f32[128,1024]{1,0:T(8,128)} copy(f32[128,1024]{1,0:T(8,128)} %get-tuple-element.13) | data formatting | bytes 1048576
  94.9 0.0 copy-done
  94.9 0.8 copy.10
Async XLA Ops:
  93.0 2.0 %copy-start = (f32[128,1024]{1,0:T(8,128)S(1)}, f32[128,1024]{1,0:T(8,128)}, u32[]{:S(2)}) copy-start(f32[128,1024]{1,0:T(8,128)} %get-tuple-element.14) | copy-start | bytes 1572868

commit v4 on v3

--- a/solution.py
+++ b/solution.py
@@ -23,14 +23,14 @@
 RING = 11
 ORDER = (
     (0, 0), (1, 0), (2, 0), (0, 1), (0, 2), (0, 3), (0, 4), (6, 1), (1, 1), (1, 2),
-    (6, 2), (1, 3), (0, 5), (1, 4), (0, 6), (7, 0), (2, 1), (6, 3), (2, 2), (0, 7),
-    (2, 3), (1, 5), (6, 4), (2, 4), (8, 0), (1, 6), (3, 0), (0, 8), (6, 5), (8, 1),
-    (1, 7), (7, 1), (2, 5), (2, 6), (8, 2), (3, 1), (0, 9), (6, 6), (4, 0), (1, 8),
-    (2, 7), (8, 3), (3, 2), (0, 10), (6, 7), (3, 3), (4, 1), (1, 9), (5, 0), (8, 4),
-    (2, 8), (3, 4), (4, 2), (1, 10), (4, 3), (8, 5), (5, 1), (3, 5), (2, 9), (3, 6),
-    (4, 4), (5, 2), (2, 10), (8, 6), (5, 3), (3, 7), (4, 5), (4, 6), (5, 4), (8, 7),
-    (7, 2), (0, 11), (3, 8), (0, 12), (0, 13), (3, 9), (4, 7), (3, 10), (5, 5), (5, 6),
-    (2, 11), (0, 14), (4, 8), (2, 12), (2, 13), (3, 11), (4, 9), (5, 7), (4, 10), (3, 12),
+    (1, 3), (0, 5), (1, 4), (0, 6), (7, 0), (6, 2), (2, 1), (2, 2), (2, 3), (1, 5),
+    (6, 3), (2, 4), (1, 6), (8, 0), (3, 0), (0, 7), (2, 5), (6, 4), (7, 1), (8, 1),
+    (2, 6), (8, 2), (4, 0), (3, 1), (0, 8), (1, 7), (6, 5), (3, 2), (0, 9), (3, 3),
+    (0, 10), (5, 0), (8, 3), (4, 1), (3, 4), (6, 6), (1, 8), (3, 5), (2, 7), (4, 2),
+    (1, 9), (8, 4), (4, 3), (3, 6), (1, 10), (6, 7), (5, 1), (4, 4), (8, 5), (2, 8),
+    (4, 5), (5, 2), (8, 6), (3, 7), (2, 9), (5, 3), (4, 6), (8, 7), (7, 2), (0, 11),
+    (2, 10), (3, 8), (5, 4), (0, 12), (5, 5), (0, 13), (4, 7), (3, 9), (5, 6), (3, 10),
+    (2, 11), (0, 14), (4, 8), (2, 12), (2, 13), (3, 11), (5, 7), (4, 9), (4, 10), (3, 12),
     (2, 14), (5, 8), (3, 13), (5, 11), (5, 9), (5, 10), (3, 14), (5, 12), (5, 13), (7, 3),
     (7, 4), (10, 0), (10, 1), (5, 14),
 )
@@ -39,7 +39,7 @@
 
 
 def kernel(
-    va_hbm, vb_hbm, loss_ref, ga_ref, gb_ref,
+    va_hbm, vb_hbm, loss_ref, rstd_ref, ga_ref, gb_ref,
     va, vb, raw, nrm, oth, swap, st_x, st_z, st_mine, st_cross,
     gp, rsy, ps, zs, rz, gf, us, u0, uf, relay, rs_same, rs_diff,
     mom, mx, mz, pc, own, ox, oz, oc2, ly, lz, lx, lsum,
@@ -546,8 +546,8 @@
         up_m = rs_diff[0, r, :].astype(f32) + rs_diff[1, r, :].astype(f32) + rs_diff[2, r, :].astype(f32)
         up_c = scale * (up_c + WIDTH * o) + d * m
         up_m = scale * (up_m + WIDTH * m) + d * o
-        grad_m = st_mine[1:2, :] * (up_m - one_m - m * two_m)
-        grad_c = st_cross[1:2, :] * (up_c - one_c - o * two_c)
+        grad_m = up_m - one_m - m * two_m
+        grad_c = up_c - one_c - o * two_c
         ga_ref[r, :] = jnp.where(first, grad_m, grad_c)
         gb_ref[r, :] = jnp.where(first, grad_c, grad_m)
         return 0
@@ -555,6 +555,8 @@
     lax.fori_loop(0, 4, finish, 0)
     gathered(lsum, lx, 4, pend["loss"])
     loss_ref[...] = lsum[0:1, 0:1]
+    rstd_ref[0:1, :] = jnp.where(first, st_mine[1:2, :], st_cross[1:2, :])
+    rstd_ref[1:2, :] = jnp.where(first, st_cross[1:2, :], st_mine[1:2, :])
     for c in sends + list(busy.values()):
         c.wait_send()
 
@@ -570,15 +572,16 @@
         )
     ] + [dma((1,))] * 11
     vmem = pl.BlockSpec(memory_space=pltpu.VMEM)
-    loss, grad_a, grad_b = pl.pallas_call(
+    loss, rstd, grad_a, grad_b = pl.pallas_call(
         kernel,
         out_shape=(
             jax.ShapeDtypeStruct((1, 1), f32),
+            jax.ShapeDtypeStruct((2, 1024), f32),
             jax.ShapeDtypeStruct((128, 1024), f32),
             jax.ShapeDtypeStruct((128, 1024), f32),
         ),
         in_specs=[pl.BlockSpec(memory_space=pltpu.HBM)] * 2,
-        out_specs=(vmem, vmem, vmem),
+        out_specs=(vmem, vmem, vmem, vmem),
         scratch_shapes=[
             vm((128, 1024), bf16), vm((128, 1024), bf16),
             vm((8, 256, 1024), bf16), vm((8, 256, 1024), bf16), vm((8, 256, 1024), bf16),
@@ -595,11 +598,11 @@
             vm((8, 8, 128), f32), vm((8, 8, 128), f32), vm((4, 8, 128), f32), vm((8, 128), f32),
         ] + sems,
         compiler_params=pltpu.CompilerParams(
-            collective_id=0, has_side_effects=True, vmem_limit_bytes=54 * 2**20
+            collective_id=0, has_side_effects=True, vmem_limit_bytes=48 * 2**20
         ),
         name="twins",
     )(view_a, view_b)
-    return loss[0, 0], grad_a, grad_b
+    return loss[0, 0], rstd[0:1] * grad_a, rstd[1:2] * grad_b
 
 
 def solution(mesh):

time: 97 us -> 95 us (0.979)
  Pallas kernels: 91.7 us -> 89.5 us
  other arithmetic: 0 us -> 1.09 us
    pallas_call x1, Pallas kernels: 91.7 us -> 89.5 us  [local(): pl.pallas_call(kernel, out_shape=(jax.ShapeDtypeStruct((1, 1), f32), jax....]
    mul x0 -> x1, other arithmetic: none -> 1.09 us  [local(): return (loss[0, 0], rstd[0:1] * grad_a, rstd[1:2] * grad_b)]
where the time goes in v4:
time: 95 us; the launch traced here: 94.9 us
  Pallas kernels  89.5 us (94%)
  between operations  2.4 us (3%)
  local copies, waits for them, and re-layouts  1.9 us (2%)
  other arithmetic  1.09 us (1%)
    pallas_call x1, Pallas kernels, local(): pl.pallas_call(kernel, out_shape=(jax.ShapeDtypeStruct((1, 1), f32), jax....  89.5 us

profile of v4, /device:TPU:1, one launch (start us, length us, event | category | flops | bytes accessed | tf_op | source)
XLA Modules:
  0.0 94.9 jit_solution(15412204482824261565)
XLA Ops:
  0.6 0.0 copy-start
  0.6 0.9 copy-done
  1.6 0.0 copy-start.1
  1.6 0.9 copy-done.1
  2.5 89.5 %twins.1 = (f32[1,1]{1,0:T(1,128)}, f32[2,1024]{1,0:T(2,128)S(1)}, f32[128,1024]{1,0:T(8,128)S(1)}, f32[128,1024]{1,0:T(8,128)S(1)}) custom-call(bf16[128,1024]{1,0:T(8,128)(2,1)S(1)} %copy-done, bf16[128,1024]{1,0:T(8,128)(2,1)S(1)} %copy-done.1), custom_call_target="tpu_custom_call" | custom-call | tf_op jit(solution)/shard_map/twins/pallas_call | solution.py:575
  92.0 1.1 %broadcast_multiply_fusion = (f32[128,1024]{1,0:T(8,128)}, f32[128,1024]{1,0:T(8,128)}) fusion(f32[128,1024]{1,0:T(8,128)S(1)} %get-tuple-element.10, f32[1024]{0:T(1024)S(1)} %bitcast.3, f32[128,1024]{1,0:T(8,128)S(1)} %get-tuple-element.9, f32[1024]{0:T(1024)S(1)} %bitcast.4), kind=kLoop, calls=%fused_computation | loop fusion | flops 262144 | bytes 2105344 | tf_op jit(solution)/shard_map/mul | solution.py:605
  (1 shorter events, 0.0 us)
Async XLA Ops:
  0.6 1.0 %copy-start = (bf16[128,1024]{1,0:T(8,128)(2,1)S(1)}, bf16[128,1024]{1,0:T(8,128)(2,1)}, u32[]{:S(2)}) copy-start(bf16[128,1024]{1,0:T(8,128)(2,1)} %va_hbm.1) | copy-start | bytes 786436
  1.6 0.9 %copy-start.1 = (bf16[128,1024]{1,0:T(8,128)(2,1)S(1)}, bf16[128,1024]{1,0:T(8,128)(2,1)}, u32[]{:S(2)}) copy-start(bf16[128,1024]{1,0:T(8,128)(2,1)} %vb_hbm.1) | copy-start | bytes 786436

commit v5 on v4

--- a/solution.py
+++ b/solution.py
@@ -23,18 +23,18 @@
 RING = 11
 ORDER = (
     (0, 0), (1, 0), (2, 0), (0, 1), (0, 2), (0, 3), (0, 4), (6, 1), (1, 1), (1, 2),
-    (1, 3), (0, 5), (1, 4), (0, 6), (7, 0), (6, 2), (2, 1), (2, 2), (2, 3), (1, 5),
-    (6, 3), (2, 4), (1, 6), (8, 0), (3, 0), (0, 7), (2, 5), (6, 4), (7, 1), (8, 1),
-    (2, 6), (8, 2), (4, 0), (3, 1), (0, 8), (1, 7), (6, 5), (3, 2), (0, 9), (3, 3),
-    (0, 10), (5, 0), (8, 3), (4, 1), (3, 4), (6, 6), (1, 8), (3, 5), (2, 7), (4, 2),
-    (1, 9), (8, 4), (4, 3), (3, 6), (1, 10), (6, 7), (5, 1), (4, 4), (8, 5), (2, 8),
-    (4, 5), (5, 2), (8, 6), (3, 7), (2, 9), (5, 3), (4, 6), (8, 7), (7, 2), (0, 11),
-    (2, 10), (3, 8), (5, 4), (0, 12), (5, 5), (0, 13), (4, 7), (3, 9), (5, 6), (3, 10),
-    (2, 11), (0, 14), (4, 8), (2, 12), (2, 13), (3, 11), (5, 7), (4, 9), (4, 10), (3, 12),
+    (0, 5), (1, 3), (1, 4), (0, 6), (7, 0), (6, 2), (2, 1), (2, 2), (1, 5), (6, 3),
+    (2, 3), (2, 4), (1, 6), (8, 0), (3, 0), (0, 7), (6, 4), (7, 1), (2, 5), (8, 1),
+    (2, 6), (8, 2), (3, 1), (0, 8), (6, 5), (4, 0), (1, 7), (3, 2), (0, 9), (8, 3),
+    (3, 3), (0, 10), (6, 6), (3, 4), (4, 1), (1, 8), (5, 0), (2, 7), (8, 4), (3, 5),
+    (4, 2), (1, 9), (6, 7), (3, 6), (4, 3), (1, 10), (4, 4), (8, 5), (5, 1), (2, 8),
+    (8, 6), (4, 5), (3, 7), (5, 2), (2, 9), (4, 6), (8, 7), (7, 2), (0, 11), (5, 3),
+    (0, 12), (2, 10), (0, 13), (5, 4), (3, 8), (5, 5), (4, 7), (3, 9), (5, 6), (3, 10),
+    (2, 11), (0, 14), (2, 12), (2, 13), (4, 8), (5, 7), (3, 11), (4, 9), (4, 10), (3, 12),
     (2, 14), (5, 8), (3, 13), (5, 11), (5, 9), (5, 10), (3, 14), (5, 12), (5, 13), (7, 3),
     (7, 4), (10, 0), (10, 1), (5, 14),
 )
-POOL = 48
+POOL = 32
 PARTS = 8
 
 
@@ -218,6 +218,8 @@
     def forward_x():
         far["x"] = forward(raw.at[2, lo, :], raw.at[1, hi, :], 3, gx_s, gx_r, xp, gx)
 
+    passed = {}
+
     def forward_z(k):
         if k >= PARTS:
             return
@@ -227,7 +229,11 @@
                 gz[e].wait_recv()
             src = raw.at[4, pl.ds(half * 128 + k * n, n), :]
             dst = raw.at[6, pl.ds((1 - half) * 128 + k * n, n), :]
-            send(src, dst, gz_s.at[4 + 2 * k + e], gz_r.at[4 + k], zp(to))
+            at = 4 + (2 * k + e) % 8
+            if at in passed:
+                passed[at].wait_send()
+                sends[:] = [c for c in sends if c is not passed[at]]
+            passed[at] = send(src, dst, gz_s.at[at], gz_r.at[4 + k], zp(to))
 
     def pass_far(k):
         n = 128 // PARTS
@@ -418,18 +424,24 @@
     tn = (((0,), (0,)), ((), ()))
     nn = (((1,), (0,)), ((), ()))
 
-    def product(i, terms, store):
+    def product(i, terms, store, after=None):
         def tile(t, _):
-            cols = pl.ds(pl.multiple_of(t * 256, 256), 256)
+            cols = pl.ds(t * 256 if after is not None else pl.multiple_of(t * 256, 256), 256)
             acc = jnp.zeros((256, 256), f32)
             for p, q, k, how in terms:
                 acc = acc + lax.dot_general(gf[p, q], oth[k, :, cols], how, preferred_element_type=f32)
             mom[0:1, cols] += jnp.sum(acc, axis=0, keepdims=True)
             mom[1:2, cols] += jnp.sum(acc * oth[i, :, cols].astype(f32), axis=0, keepdims=True)
             store(cols, acc)
+            if after is not None:
+                after(cols)
             return 0
 
-        lax.fori_loop(0, 4, tile, 0)
+        if after is None:
+            lax.fori_loop(0, 4, tile, 0)
+        else:
+            for t in range(4):
+                tile(t, 0)
 
     def upper(i):
         terms = [(i, j, 3 + j if j else 0, nn) for j in range(4) if (i, j) in UNITS and (i, j) != (3, 3)]
@@ -442,7 +454,15 @@
             if i in (1, 2):
                 uf[i - 1, :, cols] = acc
 
-        product(i, terms + [(1, 0, 1, tn)] if i == 0 else terms, store)
+        def leave(cols):
+            if i == 1:
+                send(us.at[1, pl.ds(rows_o, 128), cols], rs_diff.at[1, :, cols], None, ud_r.at[1], xq(1))
+            else:
+                send(us.at[2, pl.ds(rows_c, 128), cols], rs_same.at[1, :, cols], None, us_r.at[1], xp(3))
+
+        if i == 0:
+            terms = terms + [(1, 0, 1, tn)]
+        product(i, terms, store, leave if i in (1, 2) else None)
 
     def upper_far():
         def store(cols, acc):
@@ -475,9 +495,9 @@
             relays.append(send(us.at[3, rows_same, :], relay.at[0], rl_s.at[0], rl_r.at[0], xp(1)))
             relays.append(send(us.at[3, rows_diff, :], relay.at[1], rl_s.at[1], rl_r.at[1], xp(3)))
         elif i == 1:
-            diff.append(send(us.at[1, rows_diff, :], rs_diff.at[1], ud_s.at[1], ud_r.at[1], xq(1)))
+            diff.append(Group(rs_diff.at[1], ud_r.at[1]))
         elif i == 2:
-            same.append(send(us.at[2, rows_same, :], rs_same.at[1], us_s.at[1], us_r.at[1], xp(3)))
+            same.append(Group(rs_same.at[1], us_r.at[1]))
 
     def pass_x(k):
         start = rows_o if k else rows_c
@@ -567,7 +587,7 @@
     sems = [
         dma(shape)
         for shape in (
-            (2,), (POOL,), (2,), (6,), (4 + 2 * PARTS,), (8,), (2,), (3,), (2,),
+            (2,), (POOL,), (2,), (6,), (12,), (8,), (2,), (3,), (2,),
             (2,), (6,), (4 + PARTS,), (8,), (2,), (3,), (2,), (NU, 2), (NU,), (NU, 2),
         )
     ] + [dma((1,))] * 11

time: 95 us -> 94.2 us (level)
  no operation moved by 1% of the time
where the time goes in v5:
time: 94.2 us; the launch traced here: 94 us
  Pallas kernels  88.6 us (94%)
  between operations  2.4 us (3%)
  local copies, waits for them, and re-layouts  1.9 us (2%)
  other arithmetic  1.09 us (1%)
    pallas_call x1, Pallas kernels, local(): pl.pallas_call(kernel, out_shape=(jax.ShapeDtypeStruct((1, 1), f32), jax....  88.6 us
    unnamed x4, local copies, waits for them, and re-layouts  1.89 us

profile of v5, /device:TPU:1, one launch (start us, length us, event | category | flops | bytes accessed | tf_op | source)
XLA Modules:
  0.0 94.0 jit_solution(15930956272863281674)
XLA Ops:
  0.6 0.0 copy-start
  0.6 0.9 %copy-done = bf16[128,1024]{1,0:T(8,128)(2,1)S(1)} copy-done((bf16[128,1024]{1,0:T(8,128)(2,1)S(1)}, bf16[128,1024]{1,0:T(8,128)(2,1)}, u32[]{:S(2)}) %copy-start) | copy-done | bytes 262168
  1.6 0.0 copy-start.1
  1.6 0.9 %copy-done.1 = bf16[128,1024]{1,0:T(8,128)(2,1)S(1)} copy-done((bf16[128,1024]{1,0:T(8,128)(2,1)S(1)}, bf16[128,1024]{1,0:T(8,128)(2,1)}, u32[]{:S(2)}) %copy-start.1) | copy-done | bytes 262168
  2.5 88.6 %twins.1 = (f32[1,1]{1,0:T(1,128)}, f32[2,1024]{1,0:T(2,128)S(1)}, f32[128,1024]{1,0:T(8,128)S(1)}, f32[128,1024]{1,0:T(8,128)S(1)}) custom-call(bf16[128,1024]{1,0:T(8,128)(2,1)S(1)} %copy-done, bf16[128,1024]{1,0:T(8,128)(2,1)S(1)} %copy-done.1), custom_call_target="tpu_custom_call" | custom-call | tf_op jit(solution)/shard_map/twins/pallas_call | solution.py:595
  91.2 1.1 %broadcast_multiply_fusion = (f32[128,1024]{1,0:T(8,128)}, f32[128,1024]{1,0:T(8,128)}) fusion(f32[128,1024]{1,0:T(8,128)S(1)} %get-tuple-element.10, f32[1024]{0:T(1024)S(1)} %bitcast.3, f32[128,1024]{1,0:T(8,128)S(1)} %get-tuple-element.9, f32[1024]{0:T(1024)S(1)} %bitcast.4), kind=kLoop, calls=%fused_computation | loop fusion | flops 262144 | bytes 2105344 | tf_op jit(solution)/shard_map/mul | solution.py:625
  (1 shorter events, 0.0 us)
Async XLA Ops:
  0.6 1.0 %copy-start = (bf16[128,1024]{1,0:T(8,128)(2,1)S(1)}, bf16[128,1024]{1,0:T(8,128)(2,1)}, u32[]{:S(2)}) copy-start(bf16[128,1024]{1,0:T(8,128)(2,1)} %va_hbm.1) | copy-start | bytes 786436
  1.6 0.9 %copy-start.1 = (bf16[128,1024]{1,0:T(8,128)(2,1)S(1)}, bf16[128,1024]{1,0:T(8,128)(2,1)}, u32[]{:S(2)}) copy-start(bf16[128,1024]{1,0:T(8,128)(2,1)} %vb_hbm.1) | copy-start | bytes 786436
